TPU v7x, 32 devices: a whole 2x2x4 slice. The times are simulated.
32 devices in a mesh: group: 2 (over y), dp: 8 (over z, x), tensor: 2 (over core).
Axes of the slice: x: 2, y: 2, z: 4, core: 2. Of those that a mesh axis runs over, the one named last changes fastest.
Arguments:
- tokens: bfloat16 [12288, 2048], P(('group', 'dp')), may hold values from -6 to 6
- doc_lengths: int32 [16, 3], P(('group', 'dp')), may hold values from 1 to 480, 768 in all within a row
- cotangent: bfloat16 [12288, 2048], P(('group', 'dp')), may hold values from -6 to 6
- inner_in: float32 [2, 2048, 2, 5120], P('group', 'dp', 'tensor')
- inner_out: float32 [2, 2, 5120, 2048], P('group', 'tensor', None, 'dp')
- inner_shared: float32 [2, 2048, 267], P('group', ('dp', 'tensor'))
- first_in: float32 [2, 2048, 2, 5120], P('group', 'dp', 'tensor')
- first_out: float32 [2, 2, 5120, 2048], P('group', 'tensor', None, 'dp')
- first_shared: float32 [2, 2048, 267], P('group', ('dp', 'tensor'))
- second_in: float32 [2, 2048, 2, 5120], P('group', 'dp', 'tensor')
- second_out: float32 [2, 2, 5120, 2048], P('group', 'tensor', None, 'dp')
- second_shared: float32 [2, 2048, 267], P('group', ('dp', 'tensor'))
- outer_in: float32 [2048, 2, 5120], P('dp', 'tensor')
- outer_out: float32 [2, 5120, 2048], P('tensor', None, 'dp')
- outer_shared: float32 [2048, 267], P(('dp', 'tensor'))
- momentum_in: float32 [2048, 2, 5120], P('dp', 'tensor')
- momentum_out: float32 [2, 5120, 2048], P('tensor', None, 'dp')
- momentum_shared: float32 [2048, 267], P(('dp', 'tensor'))
Outputs:
- block_out: bfloat16 [12288, 2048], P(('group', 'dp'))
- tokens_grad: bfloat16 [12288, 2048], P(('group', 'dp'))
- clip_factors: float32 [16], replicated
- new_first_in: float32 [2, 2048, 2, 5120], P('group', 'dp', 'tensor')
- new_first_out: float32 [2, 2, 5120, 2048], P('group', 'tensor', None, 'dp')
- new_first_shared: float32 [2, 2048, 267], P('group', ('dp', 'tensor'))
- new_second_in: float32 [2, 2048, 2, 5120], P('group', 'dp', 'tensor')
- new_second_out: float32 [2, 2, 5120, 2048], P('group', 'tensor', None, 'dp')
- new_second_shared: float32 [2, 2048, 267], P('group', ('dp', 'tensor'))
- mean_delta_in: float32 [2048, 2, 5120], P('dp', 'tensor')
- mean_delta_out: float32 [2, 5120, 2048], P('tensor', None, 'dp')
- mean_delta_shared: float32 [2048, 267], P(('dp', 'tensor'))
- new_momentum_in: float32 [2048, 2, 5120], P('dp', 'tensor')
- new_momentum_out: float32 [2, 5120, 2048], P('tensor', None, 'dp')
- new_momentum_shared: float32 [2048, 267], P(('dp', 'tensor'))
- new_outer_in: float32 [2048, 2, 5120], P('dp', 'tensor')
- new_outer_out: float32 [2, 5120, 2048], P('tensor', None, 'dp')
- new_outer_shared: float32 [2048, 267], P(('dp', 'tensor'))
- copy_in: bfloat16 [2048, 2, 5120], P('dp', 'tensor')
- copy_out: bfloat16 [2, 5120, 2048], P('tensor', None, 'dp')
- copy_shared: bfloat16 [2048, 267], P(('dp', 'tensor'))
Inputs may be any that keep to these rules, and one draw needn't show every extreme that they name: `doc_lengths`: each row holds the lengths, in order, of the documents packed into one sequence slot; a row sums to 768.
All inputs are finite; a program needn't handle non-finite values.
Results may differ from a plain program's by a relative error of at most 0.024.
Values may be sent and summed in bfloat16 or wider, within the bound.
No kernel may reach another device: no remote copies, remote signals or barrier semaphores. Data moves between devices by JAX's collectives and lax.ppermute only.
A program may use at most 320 MiB of HBM per device.

v0:
```python
import jax
import jax.numpy as jnp
from jax import lax
from jax.experimental import pallas as pl
from jax.experimental.pallas import tpu as pltpu
from jax.sharding import PartitionSpec as P

HEADS = 16
HD = 128
FF = 8192
BLOCK = 256
STEP = 10

norm_eps = 1e-05
hidden_score = -1e30
shown_score = 3e38
beta_one = 0.9
beta_two = 0.95
adam_eps = 1e-08
rate_matrix = 0.02
rate_vector = 0.2
weight_decay = 0.1
outer_beta = 0.9
outer_rate = 0.7
clip_limit = 5.0
score_scale = HD ** (-0.5)
log2_e = 1.4426950408889634
correct_one = 1.0 / (1.0 - beta_one**STEP)
correct_two = 1.0 / (1.0 - beta_two**STEP)

f32 = jnp.float32
bf16 = jnp.bfloat16
ROWS = 128
LANES = 128
VMEM_LIMIT = 40 * 1024 * 1024
VMEM_MOST = 58 * 1024 * 1024


def shape(dims, dtype):
    return jax.ShapeDtypeStruct(dims, dtype)


def call(body, out_shape, grid, in_specs, out_specs, args, *, ids=(), scratch=(), aliases=None,
         flops=0, name=None, vmem=VMEM_LIMIT):
    outs = out_shape if isinstance(out_shape, (list, tuple)) else [out_shape]
    moved = sum(a.size * a.dtype.itemsize for a in args)
    moved += sum(o.size * o.dtype.itemsize for o in outs)
    return pl.pallas_call(
        body,
        out_shape=out_shape,
        grid_spec=pltpu.PrefetchScalarGridSpec(
            num_scalar_prefetch=len(ids),
            grid=grid,
            in_specs=in_specs,
            out_specs=out_specs,
            scratch_shapes=list(scratch),
        ),
        input_output_aliases={len(ids) + k: v for k, v in (aliases or {}).items()},
        compiler_params=pltpu.CompilerParams(vmem_limit_bytes=vmem),
        cost_estimate=pl.CostEstimate(flops=flops, bytes_accessed=moved, transcendentals=0),
        name=name,
    )(*ids, *args)


def pick_blocks(array, block_ids, width, count, stacked):
    rows = array.shape[0]
    if width % LANES:
        taken = jnp.take(array.reshape(rows, -1, width), block_ids, axis=1)
        return taken.transpose(1, 0, 2) if stacked else taken.reshape(rows, count * width)

    def body(ids_ref, in_ref, out_ref):
        if stacked:
            out_ref[0] = in_ref[...]
        else:
            out_ref[...] = in_ref[...]

    if stacked:
        out, spec = shape((count, rows, width), array.dtype), pl.BlockSpec(
            (1, rows, width), lambda j, ids: (j, 0, 0)
        )
    else:
        out, spec = shape((rows, count * width), array.dtype), pl.BlockSpec(
            (rows, width), lambda j, ids: (0, j)
        )
    return call(
        body, out, (count,), [pl.BlockSpec((rows, width), lambda j, ids: (0, ids[j]))], spec,
        [array], ids=[block_ids], name="pick_blocks",
    )


def columns_of(block_id, width):
    return pl.ds(pl.multiple_of(block_id * width, width), width)


def placing(array, ids, count):
    part = array.shape[1] // count
    if part % LANES == 0:
        return array, count, part
    return pick_blocks(array, ids, part, count, False), 0, part


def put_back(array, ids, count):
    part = array.shape[1] // count
    if part % LANES == 0:
        return array
    back = jnp.sum(
        jnp.where(ids[None, :] == jnp.arange(count)[:, None], jnp.arange(count)[None, :], 0), axis=1
    ).astype(jnp.int32)
    return pick_blocks(array, back, part, count, False)


def norm_stats(rows):
    mean = jnp.mean(rows, axis=-1, keepdims=True)
    centered = rows - mean
    inv = lax.rsqrt(jnp.mean(centered * centered, axis=-1, keepdims=True) + norm_eps)
    return centered * inv, inv


def row_spec(cols, rows=ROWS):
    return pl.BlockSpec((rows, cols), lambda i, *ids: (i, 0))


def turned_spec(cols, blocks):
    return pl.BlockSpec(
        (ROWS, cols), lambda i, ids, split: ((i + split[0] * (blocks // 2)) % blocks, 0)
    )


def whole_spec(rows, cols):
    return pl.BlockSpec((rows, cols), lambda i, *ids: (0, 0))


def first_norm(tokens, ids, split, gain, bias, count):
    total, width = tokens.shape
    tokens, moved, part = placing(tokens, ids, count)

    def body(ids_ref, split_ref, x_ref, g_ref, c_ref, x_out, n_out):
        for o in range(moved):
            x_out[:, o * part : (o + 1) * part] = x_ref[:, columns_of(ids_ref[o], part)]
        if not moved:
            x_out[...] = x_ref[...]
        unit, _ = norm_stats(x_out[...].astype(f32))
        n_out[...] = (unit * g_ref[...] + c_ref[...]).astype(bf16)

    return call(
        body,
        [shape((total, width), bf16)] * 2,
        (total // ROWS,),
        [turned_spec(width, total // ROWS), whole_spec(1, width), whole_spec(1, width)],
        [row_spec(width)] * 2,
        [tokens, gain, bias],
        ids=[ids, split],
        name="first_norm",
    )


def first_spec(cols, blocks):
    return pl.BlockSpec((ROWS, cols), lambda i, *ids: (jnp.minimum(i, blocks - 1), 0))


def swapped(values, part):
    if part % LANES:
        return values
    blocks = [values[:, o : o + part] for o in range(0, values.shape[1], part)]
    return jnp.concatenate([blocks[pair_of(o)] for o in range(len(blocks))], axis=1)


def pair_of(o):
    return o if o & 2 else o ^ 1


def swap_small(values, part):
    if part % LANES == 0:
        return values
    blocks = [values[:, o : o + part] for o in range(0, values.shape[1], part)]
    return jnp.concatenate([blocks[pair_of(o)] for o in range(len(blocks))], axis=1)


def cotangent_order(cotangent, ids, split, count):
    total, width = cotangent.shape
    cotangent, moved, part = placing(cotangent, ids, count)
    mine = total // ROWS // 2

    def body(ids_ref, split_ref, c_ref, c_out, pair_out, sum_out):
        for o in range(moved):
            c_out[:, o * part : (o + 1) * part] = c_ref[:, columns_of(ids_ref[o], part)]
        if not moved:
            c_out[...] = c_ref[...]
        pair_out[...] = swapped(c_out[...], part)
        add_rows(sum_out, c_out[...].astype(f32))

    return call(
        body,
        [shape((total // 2, width), bf16)] * 2 + [shape((1, width), f32)],
        (mine,),
        [turned_spec(width, total // ROWS)],
        [row_spec(width)] * 2 + [whole_spec(1, width)],
        [cotangent],
        ids=[ids, split],
        name="cotangent_order",
    )


def hidden_units(rows, weight, bias, hidden_grad):
    total, depth = rows.shape
    cols = weight.shape[1]
    high, wide, sub = 256, 1024, 256
    curve, cube = (2.0 / 3.141592653589793) ** 0.5, 0.044715

    def body(n_ref, w_ref, b_ref, dz_ref, z_out, du_out, sum_out):
        first = pl.program_id(1) == 0
        for c in range(0, wide, sub):
            at = slice(c, c + sub)
            u = jnp.dot(n_ref[...], w_ref[:, at], preferred_element_type=f32) + b_ref[:, at]
            square = u * u
            t = jnp.tanh(curve * u * (1.0 + cube * square))
            z_out[:, at] = (0.5 * u * (1.0 + t)).astype(bf16)
            slope = 0.5 * (1.0 + t) + (0.5 * curve) * u * (1.0 - t * t) * (
                1.0 + (3.0 * cube) * square
            )
            du = (slope * dz_ref[:, at].astype(f32)).astype(bf16)
            du_out[:, at] = du
            total_du = jnp.sum(du.astype(f32), axis=0, keepdims=True)
            sum_out[:, at] = jnp.where(first, total_du, sum_out[:, at] + total_du)

    tile = pl.BlockSpec((high, wide), lambda j, i: (i, j))
    line = pl.BlockSpec((1, wide), lambda j, i: (0, j))
    return call(
        body,
        [shape((total, cols), bf16)] * 2 + [shape((1, cols), f32)],
        (cols // wide, total // high),
        [
            pl.BlockSpec((high, depth), lambda j, i: (i, 0)),
            pl.BlockSpec((depth, wide), lambda j, i: (0, j)),
            line,
            tile,
        ],
        [tile, tile, line],
        [rows, weight, bias, hidden_grad],
        flops=2 * total * depth * cols,
        name="hidden_units",
    )


def add_rows(sum_ref, values):
    @pl.when(pl.program_id(0) == 0)
    def _():
        sum_ref[...] = jnp.zeros_like(sum_ref)

    sum_ref[...] += jnp.sum(values, axis=0, keepdims=True)


def middle_norm(x_rel, part_own, part_other, bias_out, gain, bias, part):
    total, width = part_other.shape

    def body(x_ref, a_ref, b_ref, bo_ref, g_ref, c_ref, h_out, n_out, pair_out):
        mid = x_ref[...].astype(f32) + (
            a_ref[...].astype(f32) + b_ref[...].astype(f32)
        ) + bo_ref[...]
        h_out[...] = mid
        unit, _ = norm_stats(mid)
        low = (unit * g_ref[...] + c_ref[...]).astype(bf16)
        n_out[...] = low
        pair_out[...] = swapped(low, part)

    return call(
        body,
        [shape((total, width), f32)] + [shape((total, width), bf16)] * 2,
        (total // ROWS,),
        [row_spec(width)] * 3 + [whole_spec(1, width)] * 3,
        [row_spec(width)] * 3,
        [x_rel, part_own, part_other, bias_out, gain, bias],
        name="middle_norm",
    )


def block_result(middle, part_own, part_pair, bias_down, ids, count):
    total, width = middle.shape
    part = width // count

    def body(ids_ref, h_ref, a_ref, p_ref, b2_ref, out_ref):
        value = a_ref[...].astype(f32) + swapped(p_ref[...], part).astype(f32)
        value = (h_ref[...] + value + b2_ref[...]).astype(bf16)
        if part % LANES:
            out_ref[...] = value
        else:
            for o in range(count):
                out_ref[:, columns_of(ids_ref[o], part)] = value[:, o * part : (o + 1) * part]

    result = call(
        body,
        shape((total, width), bf16),
        (total // ROWS,),
        [row_spec(width)] * 3 + [whole_spec(1, width)],
        row_spec(width),
        [middle, part_own, part_pair, bias_down],
        ids=[ids],
        name="block_result",
    )
    return put_back(result, ids, count)


def middle_backward(middle, part_own, part_other, part_pair, cot_rel, gain, part):
    total, width = middle.shape

    def body(h_ref, a_ref, b_ref, p_ref, dy_ref, g_ref, dh_out, low_out, gg_out, gc_out, gbo_out):
        unit, inv = norm_stats(h_ref[...])
        grad = a_ref[...].astype(f32) + b_ref[...].astype(f32)
        grad = grad + swapped(p_ref[...], part).astype(f32)
        scaled = grad * g_ref[...]
        dh = dy_ref[...].astype(f32) + inv * (
            scaled
            - jnp.mean(scaled, axis=-1, keepdims=True)
            - unit * jnp.mean(scaled * unit, axis=-1, keepdims=True)
        )
        dh_out[...] = dh
        low = dh.astype(bf16)
        low_out[...] = low
        add_rows(gg_out, grad * unit)
        add_rows(gc_out, grad)
        add_rows(gbo_out, low.astype(f32))

    vec = shape((1, width), f32)
    return call(
        body,
        [shape((total, width), f32), shape((total, width), bf16), vec, vec, vec],
        (total // ROWS,),
        [row_spec(width)] * 5 + [whole_spec(1, width)],
        [row_spec(width)] * 2 + [whole_spec(1, width)] * 3,
        [middle, part_own, part_other, part_pair, cot_rel, gain],
        name="middle_backward",
    )


def first_backward(x_rel, part_own, part_other, keyval_grad, w_keyval_t, dh, gain, ids, count):
    total, width = dh.shape
    part = width // count
    kv = keyval_grad.shape[1]

    def body(ids_ref, x_ref, a_ref, b_ref, kv_ref, w_ref, dh_ref, g_ref, t_out, gg_out, gc_out):
        unit, inv = norm_stats(x_ref[...].astype(f32))
        grad = (a_ref[...].astype(f32) + b_ref[...].astype(f32)) + jnp.dot(
            kv_ref[...], w_ref[...], preferred_element_type=f32
        )
        scaled = grad * g_ref[...]
        value = dh_ref[...] + inv * (
            scaled
            - jnp.mean(scaled, axis=-1, keepdims=True)
            - unit * jnp.mean(scaled * unit, axis=-1, keepdims=True)
        )
        low = value.astype(bf16)
        if part % LANES:
            t_out[...] = low
        else:
            for o in range(count):
                t_out[:, columns_of(ids_ref[o], part)] = low[:, o * part : (o + 1) * part]
        add_rows(gg_out, grad * unit)
        add_rows(gc_out, grad)

    vec = shape((1, width), f32)
    result, gain_grad, bias_grad = call(
        body,
        [shape((total, width), bf16), vec, vec],
        (total // ROWS,),
        [row_spec(width)] * 3
        + [row_spec(kv), whole_spec(kv, width), row_spec(width), whole_spec(1, width)],
        [row_spec(width)] + [whole_spec(1, width)] * 2,
        [x_rel, part_own, part_other, keyval_grad, w_keyval_t, dh, gain],
        ids=[ids],
        flops=2 * total * width * kv,
        name="first_backward",
    )
    return put_back(result, ids, count), gain_grad, bias_grad


TILE = 256


def score_limits(lengths, token_count, first_place):
    doc_ends = jnp.cumsum(lengths)
    doc_starts = doc_ends - lengths
    places = (jnp.arange(token_count, dtype=jnp.int32) + first_place) % token_count
    doc_ids = jnp.sum((places[:, None] >= doc_ends[None, :]).astype(jnp.int32), axis=1)
    owners = doc_ids[:, None] == jnp.arange(lengths.shape[0], dtype=jnp.int32)[None, :]
    doc_begin = jnp.sum(jnp.where(owners, doc_starts[None, :], 0), axis=1)
    blocks = (places - doc_begin) // BLOCK
    seen = (doc_ids[:, None] == doc_ids[None, :]) & (blocks[None, :] <= blocks[:, None])
    seen_t = (doc_ids[None, :] == doc_ids[:, None]) & (blocks[:, None] <= blocks[None, :])
    pick = lambda s: jnp.where(s, shown_score, hidden_score).astype(f32)
    return pick(seen), pick(seen_t)


def attention_forward(queries, key_value, limits, heads):
    total = queries.shape[0]
    tiles = total // TILE
    c = score_scale * log2_e

    def body(q_ref, kv_ref, lim_ref, o_ref, lse_ref, top_ref):
        tile, head = pl.program_id(0), pl.program_id(1)
        k = kv_ref[:, :HD]
        v = kv_ref[:, HD:]
        s = lax.dot_general(
            q_ref[...], k, (((1,), (1,)), ((), ())), preferred_element_type=f32
        )
        s = jnp.minimum(s, lim_ref[...])
        m = jnp.max(s, axis=1, keepdims=True)
        p = jnp.exp2((s - m) * c)
        l = jnp.sum(p, axis=1, keepdims=True)
        o = jnp.dot(p.astype(bf16), v, preferred_element_type=f32)
        o_ref[...] = (o / l).astype(bf16)
        lane = lax.broadcasted_iota(jnp.int32, (TILE, LANES), 1)
        lse = m * c + jnp.log2(l)
        lse_ref[...] = jnp.where(lane == head, lse, lse_ref[...])

        @pl.when((tile == 0) & (head == 0))
        def _():
            top_ref[...] = jnp.full_like(top_ref, hidden_score)

        row = lax.broadcasted_iota(jnp.int32, (heads, LANES), 0)
        best = jnp.max(m, axis=0, keepdims=True) * score_scale
        top_ref[...] = jnp.where(row == head, jnp.maximum(top_ref[...], best), top_ref[...])

    return call(
        body,
        [shape((total, heads * HD), bf16), shape((total, LANES), f32), shape((heads, LANES), f32)],
        (tiles, heads),
        [
            pl.BlockSpec((TILE, HD), lambda i, h: (i, h)),
            pl.BlockSpec((total, 2 * HD), lambda i, h: (0, 0)),
            pl.BlockSpec((TILE, total), lambda i, h: (i, 0)),
        ],
        [
            pl.BlockSpec((TILE, HD), lambda i, h: (i, h)),
            pl.BlockSpec((TILE, LANES), lambda i, h: (i, 0)),
            pl.BlockSpec((heads, LANES), lambda i, h: (0, 0)),
        ],
        [queries, key_value, limits],
        flops=8 * total * total * HD * heads,
        name="attention_forward",
    )


def attention_backward(queries, grad_att, key_value, limits_t, lse_t, dot_t, heads):
    total = queries.shape[0]
    tiles = total // TILE
    c = score_scale * log2_e

    def body(q_ref, da_ref, kv_ref, lim_ref, lse_ref, dot_ref, dq_ref, dkv_ref):
        tile, head = pl.program_id(0), pl.program_id(1)
        k = kv_ref[:, :HD]
        v = kv_ref[:, HD:]
        q = q_ref[...]
        da = da_ref[...]
        nt = (((1,), (1,)), ((), ()))
        s = lax.dot_general(k, q, nt, preferred_element_type=f32)
        s = jnp.minimum(s, lim_ref[...])
        p = jnp.exp2(s * c - lse_ref[pl.ds(head, 1), :])
        dp = lax.dot_general(v, da, nt, preferred_element_type=f32)
        ds = (p * (dp - dot_ref[pl.ds(head, 1), :])).astype(bf16)
        dq = lax.dot_general(ds, k, (((0,), (0,)), ((), ())), preferred_element_type=f32)
        dq_ref[...] = (dq * score_scale).astype(bf16)

        @pl.when((tile == 0) & (head == 0))
        def _():
            dkv_ref[...] = jnp.zeros_like(dkv_ref)

        dkv_ref[:, :HD] += jnp.dot(ds, q, preferred_element_type=f32) * score_scale
        dkv_ref[:, HD:] += jnp.dot(p.astype(bf16), da, preferred_element_type=f32)

    return call(
        body,
        [shape((total, heads * HD), bf16), shape((total, 2 * HD), f32)],
        (tiles, heads),
        [
            pl.BlockSpec((TILE, HD), lambda i, h: (i, h)),
            pl.BlockSpec((TILE, HD), lambda i, h: (i, h)),
            pl.BlockSpec((total, 2 * HD), lambda i, h: (0, 0)),
            pl.BlockSpec((total, TILE), lambda i, h: (0, i)),
            pl.BlockSpec((heads, TILE), lambda i, h: (0, i)),
            pl.BlockSpec((heads, TILE), lambda i, h: (0, i)),
        ],
        [
            pl.BlockSpec((TILE, HD), lambda i, h: (i, h)),
            pl.BlockSpec((total, 2 * HD), lambda i, h: (0, 0)),
        ],
        [queries, grad_att, key_value, limits_t, lse_t, dot_t],
        flops=20 * total * total * HD * heads,
        name="attention_backward",
    )


def adam_values(gradient, weight, one, two, rate, decay):
    new_one = beta_one * one + (1.0 - beta_one) * gradient
    new_two = beta_two * two + (1.0 - beta_two) * gradient * gradient
    direction = (new_one * correct_one) / (jnp.sqrt(new_two * correct_two) + adam_eps)
    return new_one, new_two, weight - rate * (direction + decay * weight)


def to_tiles(flat, tiles_ref):
    for j in range(8):
        tiles_ref[:, j, :] = flat[:, j * LANES : (j + 1) * LANES]


def adam_in(gradient, weight, one, two, outer, start, full):
    rows, cols = gradient.shape
    step = 64
    base = (start // 1024).reshape(1)
    tall = pl.BlockSpec((step, 8, LANES), lambda i, j, b: (i, b[0] + j, 0))
    flat = pl.BlockSpec((step, 1024), lambda i, j, b: (i, j))
    args = [gradient, weight, one, two, outer]
    specs = [flat] + [tall] * 4
    aliases = {}
    if full is not None:
        aliases = {5: 0, 6: 1}
        args += list(full)
        specs += [pl.BlockSpec(memory_space=pl.ANY)] * 2

    def body(_, g_ref, w_ref, one_ref, two_ref, out_ref, *rest):
        one_out, two_out, delta_out, grad_tiles, delta_tiles = rest[-5:]
        to_tiles(g_ref[...].astype(f32), grad_tiles)
        new_one, new_two, stepped = adam_values(
            grad_tiles[...], w_ref[...], one_ref[...], two_ref[...], rate_matrix, weight_decay
        )
        one_out[...] = new_one
        two_out[...] = new_two
        delta_tiles[...] = out_ref[...] - stepped
        for j in range(8):
            delta_out[:, j * LANES : (j + 1) * LANES] = delta_tiles[:, j, :].astype(bf16)

    whole = shape(weight.shape, f32)
    return call(
        body,
        [whole, whole, shape((rows, cols), bf16)],
        (rows // step, cols // 1024),
        specs,
        [tall, tall, flat],
        args,
        ids=[base],
        scratch=[pltpu.VMEM((step, 8, LANES), f32)] * 2,
        aliases=aliases,
        name="adam_in",
        vmem=VMEM_MOST,
    )


def adam_out(gradient, weight, one, two, outer, start, full):
    rows, cols = gradient.shape
    step = 512
    base = (start // step).reshape(1)
    tall = pl.BlockSpec((step, cols), lambda i, b: (b[0] + i, 0))
    flat = pl.BlockSpec((step, cols), lambda i, b: (i, 0))
    args = [gradient, weight, one, two, outer]
    specs = [flat] + [tall] * 4
    aliases = {}
    if full is not None:
        aliases = {5: 0, 6: 1}
        args += list(full)
        specs += [pl.BlockSpec(memory_space=pl.ANY)] * 2

    def body(_, g_ref, w_ref, one_ref, two_ref, out_ref, *rest):
        one_out, two_out, delta_out = rest[-3:]
        new_one, new_two, stepped = adam_values(
            g_ref[...].astype(f32), w_ref[...], one_ref[...], two_ref[...], rate_matrix,
            weight_decay,
        )
        one_out[...] = new_one
        two_out[...] = new_two
        delta_out[...] = (out_ref[...] - stepped).astype(bf16)

    whole = shape(weight.shape, f32)
    return call(
        body,
        [whole, whole, shape((rows, cols), bf16)],
        (rows // step,),
        specs,
        [tall, tall, flat],
        args,
        ids=[base],
        aliases=aliases,
        name="adam_out",
        vmem=VMEM_MOST,
    )


def outer_values(mean, momentum, outer):
    velocity = outer_beta * momentum + mean
    return velocity, outer - outer_rate * (mean + outer_beta * velocity)


def outer_in(both, momentum, outer, factor, start, full):
    _, rows, cols = both.shape
    step = 64
    base = (start // 1024).reshape(1)
    tall = pl.BlockSpec((step, 8, LANES), lambda i, j, b: (i, b[0] + j, 0))
    flat = pl.BlockSpec((2, step, 1024), lambda i, j, b: (0, i, j))
    wide = pl.BlockSpec((step, 1024), lambda i, j, b: (i, b[0] + j))
    args = [both, momentum, outer]
    specs = [flat, tall, tall]
    if factor is not None:
        args.append(factor)
        specs.append(pl.BlockSpec((8, LANES), lambda i, j, b: (0, 0)))
    aliases = {}
    if full is not None:
        aliases = {len(args) + k: k for k in range(4)}
        args += list(full)
        specs += [pl.BlockSpec(memory_space=pl.ANY)] * 4

    def body(_, both_ref, mom_ref, out_ref, *rest):
        mean_out, vel_out, new_out, copy_out, mean_tiles, new_tiles = rest[-6:]
        to_tiles((both_ref[0].astype(f32) + both_ref[1].astype(f32)) * 0.5, mean_tiles)
        mean = mean_tiles[...]
        velocity, fresh = outer_values(mean, mom_ref[...], out_ref[...])
        if factor is not None:
            fresh = fresh * rest[0][...][None]
        mean_out[...] = mean
        vel_out[...] = velocity
        new_out[...] = fresh
        new_tiles[...] = fresh
        for j in range(8):
            copy_out[:, j * LANES : (j + 1) * LANES] = new_tiles[:, j, :].astype(bf16)

    whole = shape(outer.shape, f32)
    return call(
        body,
        [whole, whole, whole, shape((rows, outer.shape[1] * LANES), bf16)],
        (rows // step, cols // 1024),
        specs,
        [tall, tall, tall, wide],
        args,
        ids=[base],
        scratch=[pltpu.VMEM((step, 8, LANES), f32)] * 2,
        aliases=aliases,
        name="outer_in",
        vmem=VMEM_MOST,
    )


def outer_out(both, momentum, outer, start, full):
    _, rows, cols = both.shape
    step = 512
    base = (start // step).reshape(1)
    tall = pl.BlockSpec((step, cols), lambda i, b: (b[0] + i, 0))
    flat = pl.BlockSpec((2, step, cols), lambda i, b: (0, i, 0))
    args = [both, momentum, outer]
    specs = [flat, tall, tall]
    aliases = {}
    if full is not None:
        aliases = {3 + k: k for k in range(4)}
        args += list(full)
        specs += [pl.BlockSpec(memory_space=pl.ANY)] * 4

    def body(_, both_ref, mom_ref, out_ref, *rest):
        mean_out, vel_out, new_out, copy_out = rest[-4:]
        mean = (both_ref[0].astype(f32) + both_ref[1].astype(f32)) * 0.5
        velocity, fresh = outer_values(mean, mom_ref[...], out_ref[...])
        mean_out[...] = mean
        vel_out[...] = velocity
        new_out[...] = fresh
        copy_out[...] = fresh.astype(bf16)

    whole = shape(outer.shape, f32)
    return call(
        body,
        [whole, whole, whole, shape(outer.shape, bf16)],
        (rows // step,),
        specs,
        [tall] * 4,
        args,
        ids=[base],
        aliases=aliases,
        name="outer_out",
        vmem=VMEM_MOST,
    )


class Wire:
    def __init__(self, window):
        self.window, self.landed = window, []

    def send(self, block, axis, pairs):
        if len(self.landed) >= self.window:
            block, _ = lax.optimization_barrier((block, self.landed[-self.window]))
        arrived = lax.ppermute(block, axis, pairs)
        self.landed.append(arrived)
        return arrived


class Links:
    def __init__(self, count, splits, window):
        self.levels = count.bit_length() - 1
        self.far = ([1] + [1 << b for b in range(3, self.levels)])[: self.levels - 2]
        places = range(count)
        middle = [i for i in places if (i >> 1 ^ i >> 2) & 1]
        outer = [i for i in places if i not in middle]
        self.pair = [(i, i ^ 2) for i in places]
        self.inward = [(i, i ^ 2) for i in outer]
        self.outward = [(i, i ^ 2) for i in middle]
        self.between = [(i, i ^ 6) for i in middle]
        self.beside = [[(i, i ^ mask) for i in places] for mask in self.far]
        self.mirror = [(i, i ^ 6) for i in places]
        self.cores = [(i, (i + 1) % splits) for i in range(splits)]
        self.wire = Wire(window)

    def flips(self, across):
        masks = [2, across] + self.far
        table = []
        for o in range(1 << self.levels):
            flip = 0
            for level, mask in enumerate(masks):
                if o >> level & 1:
                    flip ^= mask
            table.append(flip)
        return table

    def to_side(self, block, pairs):
        return self.wire.send(block, "dp", pairs)

    def to_middle(self, block):
        return self.wire.send(block, "dp", self.between)

    def to_far(self, block, level):
        return self.wire.send(block, "dp", self.beside[level - 2])

    def to_pair(self, block):
        return self.wire.send(block, "dp", self.pair)

    def across(self, block):
        return lax.ppermute(block, "tensor", self.cores)

    def pair_now(self, block):
        return lax.ppermute(block, "dp", self.pair)


def after(value, *earlier):
    return lax.optimization_barrier((value, *earlier))[0]


class Gathered:
    def __init__(self, links, axis, mine, other=None):
        self.links, self.axis, self.mine, self.other = links, axis, mine, other
        self.held = {}

    def join(self, *blocks):
        return jnp.concatenate(blocks, axis=self.axis)

    def near(self):
        give = self.mine if self.other is None else self.other
        self.held[0] = self.join(self.mine, self.links.to_side(give, self.links.pair))

    def inward(self):
        if self.other is not None:
            self.passed = self.links.to_side(self.mine, self.links.inward)

    def middle(self):
        if self.other is None:
            self.relay = self.direct = self.links.to_middle(self.held[0])
        else:
            self.relay = self.links.to_middle(self.join(self.other, self.passed))

    def middle_rest(self):
        self.direct = self.links.to_middle(self.held[0])

    def outward(self):
        self.relayed = self.links.to_side(self.relay, self.links.outward)

    def join_far(self):
        self.held[2] = self.direct + self.relayed

    def far(self, level, o):
        self.held[o + (1 << level)] = self.links.to_far(self.held[o], level)

    def whole(self):
        for level in range(2, self.links.levels):
            for o in range(0, 1 << level, 2):
                if o + (1 << level) not in self.held:
                    self.far(level, o)
        return self.join(*[self.held[o] for o in sorted(self.held)])


class Reduced:
    def __init__(self, links, axis, size, halved, part):
        self.links, self.axis, self.size, self.halved, self.part = links, axis, size, halved, part
        self.landed = {}

    def pair_sum(self, o):
        total = self.part(o, 2)
        for block in self.landed.pop(o, []):
            total = total + block.astype(f32)
        return total.astype(bf16)

    def one(self, block, o):
        return lax.slice_in_dim(
            block, o * self.size, (o + 1) * self.size, axis=self.axis
        ).astype(f32)

    def far(self):
        sent = []
        for level in range(self.links.levels - 1, 1, -1):
            for o in reversed(range(1 << level, 2 << level, 2)):
                sent.append(self.pair_sum(o))
                arrived = self.links.to_far(sent[-1], level)
                self.landed.setdefault(o - (1 << level), []).append(arrived)
        return sent

    def inward(self):
        self.ahead = self.pair_sum(2)
        self.passed = self.links.to_side(self.ahead, self.links.inward)
        return self.ahead

    def middle(self):
        self.direct = self.links.to_middle(
            self.ahead if self.halved else self.ahead + self.passed
        )

    def middle_rest(self):
        self.relay = self.links.to_middle(self.passed)

    def single(self, o):
        total = self.part(o, 1)
        for block in self.landed[0] + [self.direct]:
            total = total + self.one(block, o)
        return total

    def near(self):
        value = self.single(1).astype(bf16)
        self.theirs = self.links.to_side(value, self.links.pair).astype(f32)
        return value

    def outward(self):
        value = self.one(self.relay, 1).astype(bf16)
        self.last = self.links.to_side(value, self.links.outward).astype(f32)

    def result(self):
        if not self.halved:
            return self.single(0) + self.theirs, None
        return self.single(0) + self.last, self.theirs + self.one(self.relay, 0)


def local(
    tokens,
    doc_lengths,
    cotangent,
    inner_in,
    inner_out,
    inner_shared,
    first_in,
    first_out,
    first_shared,
    second_in,
    second_out,
    second_shared,
    outer_in_w,
    outer_out_w,
    outer_shared,
    momentum_in,
    momentum_out,
    momentum_shared,
):
    splits = lax.axis_size("tensor")
    count = lax.axis_size("dp")
    split = lax.axis_index("tensor")
    place = lax.axis_index("dp")
    total, width = tokens.shape
    part = width // count
    local_cols = inner_in.shape[3]
    shared_cols = inner_shared.shape[2]
    heads = HEADS // splits
    qcols = heads * HD
    hidden = local_cols - qcols
    vec = 2 * HD
    own_cols = part // splits
    mine = total // 2

    links = Links(count, splits, 4)
    across = links.across
    levels = links.levels
    side = ((place >> 1) ^ (place >> 2)) & 1
    from_outer, from_middle = (jnp.array(links.flips(m), jnp.int32) for m in (4, 6))
    ids = (place ^ jnp.where(side == 0, from_outer, from_middle)).astype(jnp.int32)
    swap_group = [(0, 1), (1, 0)]
    split_id = split.astype(jnp.int32).reshape(1)

    def tall(array):
        return array.reshape(part, local_cols // LANES, LANES)

    w_in = tall(inner_in)
    w_out = inner_out.reshape(local_cols, part)
    shared_rows = lax.all_gather(inner_shared[0], ("dp", "tensor"), axis=0, tiled=True)

    half = hidden // 2
    flat_in = inner_in.reshape(part, local_cols)

    def sides(low, high):
        return (
            jnp.where(side == 0, low, high).astype(bf16),
            jnp.where(side == 0, high, low).astype(bf16),
        )

    block_q = flat_in[:, :qcols].astype(bf16)
    block_o = w_out[:qcols].astype(bf16)
    up_sides = sides(flat_in[:, qcols : qcols + half], flat_in[:, qcols + half :])
    down_sides = sides(w_out[qcols : qcols + half], w_out[qcols + half :])
    got_query = Gathered(links, 0, block_q)
    got_attn = Gathered(links, 1, block_o)
    got_up = Gathered(links, 0, *up_sides)
    got_down = Gathered(links, 1, *down_sides)
    shared_t = shared_rows.T
    shared_rel = pick_blocks(shared_t, ids, part, count, False)
    w_keyval_t = shared_rel[:vec].astype(bf16)
    vectors_t, vectors = shared_t[vec:], shared_rel[vec:]
    gain_one, bias_one, gain_two, bias_two = (vectors[k : k + 1] for k in range(4))
    bias_out, bias_down = vectors[5:6], vectors[6:7]
    bias_query = lax.dynamic_slice_in_dim(vectors_t[4], split * qcols, qcols)
    bias_up = lax.dynamic_slice_in_dim(
        vectors_t[7:].reshape(FF), split * hidden + side * half, half
    )

    nt = (((1,), (1,)), ((), ()))
    tn = (((0,), (0,)), ((), ()))

    def mm(a, b, dims=(((1,), (0,)), ((), ()))):
        return lax.dot_general(a, b, dims, preferred_element_type=f32)

    def block(array, o, blocks):
        return array[:, o * part : (o + blocks) * part]

    def both_rows(rows):
        return lax.all_gather(rows, "tensor", axis=0, tiled=True)

    def far(weight, o):
        if levels == 3:
            weight.far(2, o)

    cot_own, cot_pair, grad_bias_down = cotangent_order(cotangent, ids, split_id, count)
    got_query.near()
    got_attn.near()
    got_query.middle()
    far(got_query, 0)
    got_down.near()
    got_down.inward()
    got_attn.middle()
    far(got_attn, 0)
    got_query.outward()
    got_query.join_far()
    far(got_query, 2)
    got_attn.outward()
    got_attn.join_far()
    got_down.middle()
    got_up.near()
    far(got_attn, 2)
    w_query = got_query.whole()
    w_attn = got_attn.whole()
    got_up.inward()
    far(got_down, 0)
    cot_theirs = links.to_pair(swap_small(cot_pair, part))
    got_down.outward()
    got_down.middle_rest()
    got_down.join_far()
    far(got_up, 0)
    got_up.middle()
    far(got_down, 2)
    w_down = got_down.whole()
    got_up.outward()
    got_up.middle_rest()
    got_up.join_far()

    x_rel, normed = first_norm(tokens, ids, split_id, gain_one, bias_one, count)
    limits, limits_t = score_limits(doc_lengths[0], total, split * mine)
    key_value = mm(normed, w_keyval_t, nt).astype(bf16)
    queries = (mm(normed, w_query) + bias_query).astype(bf16)
    attended, log_totals, tops = attention_forward(queries, key_value, limits, heads)
    attn_give = mm(attended[mine:], w_attn).astype(bf16)
    attn_keep = mm(attended[:mine], w_attn).astype(bf16)
    attn_other = across(attn_give)
    middle, normed_two, normed_pair = middle_norm(
        x_rel, attn_keep, attn_other, bias_out, gain_two, bias_two, part
    )
    normed_theirs = links.to_pair(swap_small(normed_pair, part))
    far(got_up, 2)
    w_up = got_up.whole()
    normed_all = both_rows(jnp.concatenate([normed_two, normed_theirs], axis=0))
    cot_all = both_rows(jnp.concatenate([cot_own, cot_theirs], axis=0))
    hidden_grad = mm(cot_all, w_down, nt).astype(bf16)
    acts, grad_pre, grad_bias_up = hidden_units(normed_all, w_up, bias_up[None], hidden_grad)

    links.wire.window = 1 << 30
    sum_down = Reduced(
        links, 1, part, True, lambda o, b: mm(acts, block(cot_all, o, b), tn)
    )
    sum_up = Reduced(
        links, 0, part, True, lambda o, b: mm(block(normed_all, o, b), grad_pre, tn)
    )
    sent_down = sum_down.far()
    w_up_late = after(w_up, *sent_down)
    pre_give = lax.dynamic_slice_in_dim(grad_pre, (1 - split) * 2 * mine, 2 * mine)
    pre_keep = lax.dynamic_slice_in_dim(grad_pre, split * 2 * mine, 2 * mine)
    two_give = mm(pre_give, w_up_late, nt).astype(bf16)
    two_other = across(two_give)
    two_keep = mm(pre_keep, after(w_up_late, two_give), nt).astype(bf16)
    two_theirs = two_keep[mine:].astype(f32) + two_other[mine:].astype(f32)
    two_pair = links.pair_now(swap_small(two_theirs.astype(bf16), part))
    sent_up = sum_up.far()
    sum_down.inward()
    sum_down.middle()
    dh, dh_mine, grad_gain_two, grad_bias_two, grad_bias_out = middle_backward(
        middle, two_keep, two_other, two_pair, cot_own, gain_two, part
    )
    dh_low = jnp.concatenate([dh_mine, across(dh_mine)], axis=0)

    grad_att = mm(dh_low, after(w_attn, *sent_up), nt).astype(bf16)
    dots = jnp.sum(
        (grad_att.astype(f32) * attended.astype(f32)).reshape(total, heads, HD), axis=2
    )
    grad_queries, kv_part = attention_backward(
        queries, grad_att, key_value, limits_t, log_totals.T[:heads], dots.T, heads
    )
    sum_down.middle_rest()
    sum_down.near()
    sum_down.outward()
    sum_attn = Reduced(
        links, 1, part, False, lambda o, b: mm(attended, block(dh_low, o, b), tn)
    )
    sent_attn = sum_attn.far()
    one_give = mm(grad_queries[mine:], w_query, nt).astype(bf16)
    one_other = across(one_give)
    one_keep = mm(grad_queries[:mine], w_query, nt).astype(bf16)
    kv_low = (kv_part[:mine] + across(kv_part[mine:])).astype(bf16)
    grad_keyval_t = mm(kv_low, normed[:mine], tn)
    sum_up.inward()
    sum_up.middle()
    sum_query = Reduced(
        links, 0, part, False, lambda o, b: mm(block(normed, o, b), grad_queries, tn)
    )
    sum_query.far()
    sum_up.middle_rest()
    grad_mine, grad_gain_one, grad_bias_one = first_backward(
        x_rel, one_keep, one_other, kv_low, w_keyval_t, dh, gain_one, ids, count
    )
    tokens_grad = both_rows(grad_mine)

    down_part = mm(after(acts, *sent_attn), w_down).astype(bf16)
    down_sum = lax.psum_scatter(down_part, "tensor", scatter_dimension=0, tiled=True)

    peers = across(after(tops, *sent_up))
    peak = jnp.where(
        split == 0, jnp.concatenate([tops, peers]), jnp.concatenate([peers, tops])
    )
    peak = jnp.maximum(peak, lax.ppermute(peak, "group", swap_group))
    for pairs in [links.pair, links.mirror] + links.beside:
        peak = jnp.maximum(peak, lax.ppermute(peak, "dp", pairs))
    clip_rows = clip_limit / jnp.maximum(peak, clip_limit)

    sum_up.near()
    sum_up.outward()
    sum_attn.inward()
    sum_attn.middle()
    sum_query.inward()
    down_pair = links.to_pair(swap_small(down_sum[mine:], part))
    block_out = both_rows(
        block_result(middle, down_sum, down_pair, bias_down, ids, count)
    )

    grad_bias_query = jnp.sum(grad_queries.astype(f32), axis=0)
    spread = jnp.concatenate(
        [
            lax.dynamic_update_slice_in_dim(
                jnp.zeros((width,), f32), grad_bias_query, split * qcols, 0
            ),
            lax.dynamic_update_slice_in_dim(
                jnp.zeros((FF,), f32), grad_bias_up[0], split * hidden + side * half, 0
            ),
        ]
    ).reshape(1 + FF // width, width)
    near = jnp.concatenate(
        [grad_keyval_t, grad_gain_one, grad_bias_one, grad_gain_two, grad_bias_two, grad_bias_out,
         grad_bias_down],
        axis=0,
    )
    steps = jnp.arange(count, dtype=jnp.int32)
    turned = jnp.where((side == 0) & ((steps & 2) != 0), steps ^ 1, steps)
    mirrored = (place ^ from_middle).astype(jnp.int32)

    def pieces(core):
        a = pick_blocks(near, turned * splits + core, own_cols, count, True)
        b = pick_blocks(spread, mirrored * splits + core, own_cols, count, True)
        return jnp.concatenate([a[:, : vec + 4], b[:, :1], a[:, vec + 4 :], b[:, 1:]], axis=1)

    red_shared = pieces(split) + across(pieces(1 - split))
    sum_query.middle()
    sum_attn.near()
    for pairs in reversed([links.pair, links.mirror] + links.beside):
        keep = red_shared.shape[0] // 2
        red_shared = red_shared[:keep] + links.to_side(red_shared[keep:], pairs)
    red_shared = red_shared[0]
    sum_query.near()
    red_down, red_up = sum_down.result(), sum_up.result()
    red_attn, red_query = sum_attn.result()[0], sum_query.result()[0]

    one_in, two_in = tall(first_in), tall(second_in)
    one_out, two_out = (a.reshape(local_cols, part) for a in (first_out, second_out))
    base_in, mom_in = tall(outer_in_w), tall(momentum_in)
    base_out, mom_out = (a.reshape(local_cols, part) for a in (outer_out_w, momentum_out))
    clip_own = lax.dynamic_slice_in_dim(clip_rows, split * heads, heads)

    starts = [qcols + side * half, qcols + (1 - side) * half]
    zero = jnp.zeros((), jnp.int32)
    gathered = []

    def groups(delta):
        both = lax.all_gather(after(delta, *gathered[-1:]), "group", axis=0)
        gathered.append(both)
        return both

    full_in = full_out = new_in = new_out = None
    for s, gradient in zip(starts, red_down):
        *full_out, delta = adam_out(gradient, w_out, one_out, two_out, base_out, s, full_out)
        new_out = outer_out(groups(delta), mom_out, base_out, s, new_out)
    for s, gradient in zip(starts, red_up):
        *full_in, delta = adam_in(gradient, w_in, one_in, two_in, base_in, s, full_in)
        new_in = outer_in(groups(delta), mom_in, base_in, None, s, new_in)
    red_query = after(red_query, new_in[0], new_out[0])
    *full_out, delta = adam_out(red_attn, w_out, one_out, two_out, base_out, zero, full_out)
    new_out = outer_out(groups(delta), mom_out, base_out, zero, new_out)
    *full_in, delta = adam_in(red_query, w_in, one_in, two_in, base_in, zero, full_in)
    both = jnp.stack([delta, lax.ppermute(delta, "group", swap_group)])
    new_in = outer_in(both, mom_in, base_in, clip_own, zero, new_in)

    ids_col = jnp.arange(shared_cols, dtype=jnp.int32)[:, None]
    one_sh, two_sh, stepped = adam_values(
        red_shared,
        inner_shared[0].T,
        first_shared[0].T,
        second_shared[0].T,
        jnp.where(ids_col < vec, rate_matrix, rate_vector),
        jnp.where(ids_col < vec, weight_decay, 0.0),
    )
    base_sh = outer_shared.T
    delta = (base_sh - stepped).astype(bf16)
    mean_sh = (delta.astype(f32) + lax.ppermute(delta, "group", swap_group).astype(f32)) * 0.5
    vel_sh, fresh_sh = outer_values(mean_sh, momentum_shared.T, base_sh)
    row_ids = (place * splits + split) * own_cols + jnp.arange(own_cols, dtype=jnp.int32)
    clip_vec = clip_rows[:, 0]
    row_clip = jnp.sum(
        jnp.where((row_ids // HD)[None, :] == jnp.arange(HEADS)[:, None], clip_vec[:, None], 0.0),
        axis=0,
    )
    fresh_sh = fresh_sh * jnp.where(ids_col == vec + 4, row_clip[None, :], 1.0)

    shape_in, shape_out = (part, 1, local_cols), (1, local_cols, part)
    mean_in, vel_in, fresh_in, copy_in = new_in
    mean_out, vel_out, fresh_out, copy_out = new_out
    return (
        block_out,
        tokens_grad,
        clip_vec,
        full_in[0].reshape((1,) + shape_in),
        full_out[0].reshape((1,) + shape_out),
        one_sh.T[None],
        full_in[1].reshape((1,) + shape_in),
        full_out[1].reshape((1,) + shape_out),
        two_sh.T[None],
        mean_in.reshape(shape_in),
        mean_out.reshape(shape_out),
        mean_sh.T,
        vel_in.reshape(shape_in),
        vel_out.reshape(shape_out),
        vel_sh.T,
        fresh_in.reshape(shape_in),
        fresh_out.reshape(shape_out),
        fresh_sh.T,
        copy_in.reshape(shape_in),
        copy_out.reshape(shape_out),
        fresh_sh.T.astype(bf16),
    )


def solution(mesh):
    rows = P(("group", "dp"), None)
    inner = [P("group", "dp", "tensor", None), P("group", "tensor", None, "dp"),
             P("group", ("dp", "tensor"), None)]
    outer = [P("dp", "tensor", None), P("tensor", None, "dp"), P(("dp", "tensor"), None)]
    in_specs = tuple([rows] * 3 + inner * 3 + outer * 2)
    out_specs = tuple([rows] * 2 + [P()] + inner * 2 + outer * 4)
    return jax.shard_map(local, mesh=mesh, in_specs=in_specs, out_specs=out_specs, check_vma=False)
```

profile of v0, /device:TPU:0, one launch (start us, length us, event | category | flops | bytes accessed | tf_op | source)
XLA Modules:
  0.0 1109.2 jit_solution(14709807597232093259)
XLA Ops:
  18.7 8.7 collective-permute-done
  39.9 23.6 %collective-permute-done.2 = bf16[2048,256]{1,0:T(8,128)(2,1)} collective-permute-done((bf16[2048,256]{1,0:T(8,128)(2,1)}, bf16[2048,256]{1,0:T(8,128)(2,1)}, u32[]{:S(2)}, u32[]{:S(2)}) %collective-permute-start.2) | collective-permute-done | bytes 1048608 | tf_op jit(solution)/shard_map/ppermute | solution.py:683
  70.2 13.6 %collective-permute-done.5 = bf16[1024,256]{1,0:T(8,128)(2,1)} collective-permute-done((bf16[1024,256]{1,0:T(8,128)(2,1)}, bf16[1024,256]{1,0:T(8,128)(2,1)}, u32[]{:S(2)}, u32[]{:S(2)}) %collective-permute-start.5) | collective-permute-done | bytes 524320 | tf_op jit(solution)/shard_map/ppermute | solution.py:683
  92.5 11.6 %collective-permute-done.3 = bf16[512,1024]{1,0:T(8,128)(2,1)} collective-permute-done((bf16[512,1024]{1,0:T(8,128)(2,1)}, bf16[512,1024]{1,0:T(8,128)(2,1)}, u32[]{:S(2)}, u32[]{:S(2)}) %collective-permute-start.3) | collective-permute-done | bytes 1048608 | tf_op jit(solution)/shard_map/ppermute | solution.py:683
  118.1 12.5 %collective-permute-done.14 = bf16[256,2048]{1,0:T(8,128)(2,1)} collective-permute-done((bf16[256,2048]{1,0:T(8,128)(2,1)}, bf16[256,2048]{1,0:T(8,128)(2,1)}, u32[]{:S(2)}, u32[]{:S(2)}) %collective-permute-start.14) | collective-permute-done | bytes 1048608 | tf_op jit(solution)/shard_map/ppermute | solution.py:683
  140.7 12.3 %collective-permute-done.9 = bf16[1024,512]{1,0:T(8,128)(2,1)S(1)} collective-permute-done((bf16[1024,512]{1,0:T(8,128)(2,1)}, bf16[1024,512]{1,0:T(8,128)(2,1)S(1)}, u32[]{:S(2)}, u32[]{:S(2)}) %collective-permute-start.9) | collective-permute-done | bytes 1048608 | tf_op jit(solution)/shard_map/ppermute | solution.py:683
  173.9 9.9 collective-permute-done.15
  187.3 6.7 add_convert_fusion.3.q_ref
  196.8 16.2 %attention_forward.1 = (bf16[768,1024]{1,0:T(8,128)(2,1)S(1)}, f32[768,128]{1,0:T(8,128)S(1)}, f32[8,128]{1,0:T(8,128)S(1)}) custom-call(bf16[768,1024]{1,0:T(8,128)(2,1)S(1)} %add_convert_fusion.3.q_ref, bf16[768,256]{1,0:T(8,128)(2,1)S(1)} %convolution_convert_fusion.17.kv_ref, f32[768,768]{1,0:T(8,128)S(1)} %copy-done.23), custom_call_target="tpu_custom_call" | custom-call | flops 4831838208 | bytes 6295552 | tf_op jit(solution)/shard_map/attention_forward/pallas_call | solution.py:48
  232.8 34.4 %collective-permute-start.17 = (bf16[384,2048]{1,0:T(8,128)(2,1)S(1)}, bf16[384,2048]{1,0:T(8,128)(2,1)S(1)}, u32[]{:S(2)}, u32[]{:S(2)}) collective-permute-start(bf16[384,2048]{1,0:T(8,128)(2,1)S(1)} %get-tuple-element.138), channel_id=1, source_target_pairs={{0,4},{2,6},{4,0},{6,2},{8,12},{10,14},{12,8},{14,10},{1,5},{3,7},... | collective-permute-start | bytes 4718600 | tf_op jit(solution)/shard_map/ppermute | solution.py:683
  276.2 33.0 %collective-permute-done.17 = bf16[384,2048]{1,0:T(8,128)(2,1)S(1)} collective-permute-done((bf16[384,2048]{1,0:T(8,128)(2,1)S(1)}, bf16[384,2048]{1,0:T(8,128)(2,1)S(1)}, u32[]{:S(2)}, u32[]{:S(2)}) %collective-permute-start.17) | collective-permute-done | bytes 1572896 | tf_op jit(solution)/shard_map/ppermute | solution.py:683
  328.3 36.8 %collective-permute-done.25 = bf16[2048,512]{1,0:T(8,128)(2,1)} collective-permute-done((bf16[2048,512]{1,0:T(8,128)(2,1)}, bf16[2048,512]{1,0:T(8,128)(2,1)}, u32[]{:S(2)}, u32[]{:S(2)}) %collective-permute-start.25) | collective-permute-done | bytes 2097184 | tf_op jit(solution)/shard_map/ppermute | solution.py:683
  378.3 19.0 %convolution_convert_fusion.1.dz_ref = bf16[1536,2048]{1,0:T(8,128)(2,1)} fusion(bf16[1536,2048]{1,0:T(8,128)(2,1)} %all-gather.19.cloned.1.call-done, bf16[2048,2048]{1,0:T(8,128)(2,1)} %constant_dynamic-update-slice_fusion.15), kind=kOutput, calls=%fused_computation.1 | convolution fusion | flops 12888047616 | bytes 20971520 | tf_op jit(solution)/shard_map/dot_general | solution.py:922
  397.3 23.1 %collective-permute-done.26 = bf16[512,2048]{1,0:T(8,128)(2,1)} collective-permute-done((bf16[512,2048]{1,0:T(8,128)(2,1)}, bf16[512,2048]{1,0:T(8,128)(2,1)}, u32[]{:S(2)}, u32[]{:S(2)}) %collective-permute-start.26) | collective-permute-done | bytes 2097184 | tf_op jit(solution)/shard_map/ppermute | solution.py:683
  423.5 28.2 %hidden_units.1 = (bf16[1536,2048]{1,0:T(8,128)(2,1)S(1)}, bf16[1536,2048]{1,0:T(8,128)(2,1)S(1)}, f32[1,2048]{1,0:T(1,128)S(1)}) custom-call(bf16[1536,2048]{1,0:T(8,128)(2,1)} %all-gather.17.cloned.1.call-done.n_ref, bf16[2048,2048]{1,0:T(8,128)(2,1)} %constant_dynamic-update-slice_fusion.10.w_ref, f32[1,2048]{1,0:T(1,128)S(1)} %bitcast.189, ...), custom_call_target="tpu_custom_call" | custom-call | flops 12884901888 | bytes 33570816 | tf_op jit(solution)/shard_map/hidden_units/pallas_call | solution.py:48
  451.8 6.3 convolution_convert_fusion.7
  459.7 44.1 %collective-permute-done.51 = bf16[2048,512]{1,0:T(8,128)(2,1)S(1)} collective-permute-done((bf16[2048,512]{1,0:T(8,128)(2,1)S(1)}, bf16[2048,512]{1,0:T(8,128)(2,1)S(1)}, u32[]{:S(2)}, u32[]{:S(2)}) %collective-permute-start.51) | collective-permute-done | bytes 2097184 | tf_op jit(solution)/shard_map/ppermute | solution.py:683
  503.8 6.1 add_convert_fusion
  514.0 8.2 convolution_convert_fusion.6
  528.8 25.2 %collective-permute-done.54 = bf16[2048,512]{1,0:T(8,128)(2,1)} collective-permute-done((bf16[2048,512]{1,0:T(8,128)(2,1)}, bf16[2048,512]{1,0:T(8,128)(2,1)}, u32[]{:S(2)}, u32[]{:S(2)}) %collective-permute-start.54) | collective-permute-done | bytes 2097184 | tf_op jit(solution)/shard_map/ppermute | solution.py:683
  556.0 10.2 convolution_convert_fusion.3
  570.7 6.0 add_convert_fusion.1
  586.0 10.1 convolution_convert_fusion.2.a_ref
  600.4 24.5 %collective-permute-start.28 = (bf16[384,2048]{1,0:T(8,128)(2,1)}, bf16[384,2048]{1,0:T(8,128)(2,1)}, u32[]{:S(2)}, u32[]{:S(2)}) collective-permute-start(bf16[384,2048]{1,0:T(8,128)(2,1)} %add_convert_fusion.2), channel_id=1, source_target_pairs={{0,4},{2,6},{4,0},{6,2},{8,12},{10,14},{12,8},{14,10},{1,5},{3,7},... | collective-permute-start | bytes 4718600 | tf_op jit(solution)/shard_map/ppermute | solution.py:731
  636.8 7.2 adam_out.3
  644.3 6.8 fusion.9
  651.1 20.9 %collective-permute-start.53 = (bf16[2048,256]{1,0:T(8,128)(2,1)}, bf16[2048,256]{1,0:T(8,128)(2,1)}, u32[]{:S(2)}, u32[]{:S(2)}) collective-permute-start(bf16[2048,256]{1,0:T(8,128)(2,1)} %fusion.9), channel_id=1, source_target_pairs={{0,4},{2,6},{4,0},{6,2},{8,12},{10,14},{12,8},{14,10},{1,5},{3,7},... | collective-permute-start | bytes 3145736 | tf_op jit(solution)/shard_map/ppermute | solution.py:683
  672.0 5.8 middle_backward.1
  677.9 9.1 convolution_convert_fusion.4
  693.7 7.2 adam_out.4
  711.6 22.9 %collective-permute-done.43 = bf16[512,2048]{1,0:T(8,128)(2,1)} collective-permute-done((bf16[512,2048]{1,0:T(8,128)(2,1)}, bf16[512,2048]{1,0:T(8,128)(2,1)}, u32[]{:S(2)}, u32[]{:S(2)}) %collective-permute-start.43) | collective-permute-done | bytes 2097184 | tf_op jit(solution)/shard_map/ppermute | solution.py:683
  739.7 10.6 adam_in.3
  750.4 18.8 %convolution_convert_fusion = bf16[1536,2048]{1,0:T(8,128)(2,1)} fusion(bf16[1536,2048]{1,0:T(8,128)(2,1)} %copy-done.59, bf16[2048,2048]{1,0:T(8,128)(2,1)} %constant_dynamic-update-slice_fusion.15), kind=kOutput, calls=%fused_computation | convolution fusion | flops 12888047616 | bytes 20971520 | tf_op jit(solution)/shard_map/dot_general | solution.py:922
  769.4 6.6 fusion.8
  781.0 20.2 %collective-permute-done.46 = bf16[256,2048]{1,0:T(8,128)(2,1)} collective-permute-done((bf16[256,2048]{1,0:T(8,128)(2,1)}, bf16[256,2048]{1,0:T(8,128)(2,1)}, u32[]{:S(2)}, u32[]{:S(2)}) %collective-permute-start.46) | collective-permute-done | bytes 1048608 | tf_op jit(solution)/shard_map/ppermute | solution.py:683
  804.9 5.6 convolution_convert_fusion.12.da_ref
  824.2 26.2 %attention_backward.1 = (bf16[768,1024]{1,0:T(8,128)(2,1)S(1)}, f32[768,256]{1,0:T(8,128)S(1)}) custom-call(bf16[768,1024]{1,0:T(8,128)(2,1)S(1)} %copy-done.61, bf16[768,1024]{1,0:T(8,128)(2,1)S(1)} %copy-done.32, bf16[768,256]{1,0:T(8,128)(2,1)S(1)} %copy-done.58, f32[768,768]{1,0:T(8,128)S(1)} %copy-done.22, f32[8,768]{1,0:T(8,128)S(1)} %slice.362.lse_ref, ...), custom_call_target="tpu_custom_call" | custom-call | flops 12079595520 | bytes 8306688 | tf_op jit(solution)/shard_map/attention_backward/pallas_call | solution.py:48
  852.5 10.6 adam_in.4
  889.9 15.2 %collective-permute-done.59 = bf16[1024,512]{1,0:T(8,128)(2,1)} collective-permute-done((bf16[1024,512]{1,0:T(8,128)(2,1)}, bf16[1024,512]{1,0:T(8,128)(2,1)}, u32[]{:S(2)}, u32[]{:S(2)}) %collective-permute-start.59) | collective-permute-done | bytes 1048608 | tf_op jit(solution)/shard_map/ppermute | solution.py:683
  916.5 22.5 %collective-permute-start.61 = (bf16[1024,256]{1,0:T(8,128)(2,1)}, bf16[1024,256]{1,0:T(8,128)(2,1)}, u32[]{:S(2)}, u32[]{:S(2)}) collective-permute-start(bf16[1024,256]{1,0:T(8,128)(2,1)} %fusion.21), channel_id=1, source_target_pairs={{0,4},{2,6},{4,0},{6,2},{8,12},{10,14},{12,8},{14,10},{1,5},{3,7},... | collective-permute-start | bytes 1572872 | tf_op jit(solution)/shard_map/ppermute | solution.py:683
  985.5 20.2 %collective-permute-done.30.p_ref = bf16[384,2048]{1,0:T(8,128)(2,1)} collective-permute-done((bf16[384,2048]{1,0:T(8,128)(2,1)}, bf16[384,2048]{1,0:T(8,128)(2,1)}, u32[]{:S(2)}, u32[]{:S(2)}) %collective-permute-start.30) | collective-permute-done | bytes 1572896 | tf_op jit(solution)/shard_map/ppermute | solution.py:683
  1023.3 6.8 collective-permute-done.63
  1033.4 6.2 outer_out.3
  1044.2 6.2 outer_out.4
  1050.4 8.7 outer_in.3
  1059.1 8.7 outer_in.4
  1067.8 6.1 adam_in.5
  1078.4 5.7 collective-permute-done.67
  (464 shorter events, 376.7 us)
Async XLA Ops:
  8.0 153.9 %all-gather.25.cloned.1.call-start = ((), (), s32[]{:S(2)}) async-start(), calls=%async_computation.6 | async-start | bytes 2367488 | tf_op jit(solution)/shard_map/all_gather | solution.py:888
  35.4 342.9 %all-gather.19.cloned.1.call-start = ((), (), s32[]{:S(2)}) async-start(), calls=%async_computation.2 | async-start | bytes 9437184 | tf_op jit(solution)/shard_map/all_gather | solution.py:928
  37.7 46.0 %collective-permute-start.5 = (bf16[1024,256]{1,0:T(8,128)(2,1)}, bf16[1024,256]{1,0:T(8,128)(2,1)}, u32[]{:S(2)}, u32[]{:S(2)}) collective-permute-start(bf16[1024,256]{1,0:T(8,128)(2,1)} %get-tuple-element.318), channel_id=1, source_target_pairs={{0,4},{2,6},{4,0},{6,2},{8,12},{10,14},{12,8},{14,10},{1,5},{3,7},... | collective-permute-start | bytes 1572872 | tf_op jit(solution)/shard_map/ppermute | solution.py:683
  63.6 40.6 %collective-permute-start.3 = (bf16[512,1024]{1,0:T(8,128)(2,1)}, bf16[512,1024]{1,0:T(8,128)(2,1)}, u32[]{:S(2)}, u32[]{:S(2)}) collective-permute-start(bf16[512,1024]{1,0:T(8,128)(2,1)} %collective-permute-done.1), channel_id=1, source_target_pairs={{4,0},{6,2},{8,12},{10,14},{5,1},{7,3},{9,13},{11,15},{20,16},{22,... | collective-permute-start | bytes 3145736 | tf_op jit(solution)/shard_map/ppermute | solution.py:683
  68.7 40.3 %collective-permute-start.4 = (bf16[512,1024]{1,0:T(8,128)(2,1)}, bf16[512,1024]{1,0:T(8,128)(2,1)}, u32[]{:S(2)}, u32[]{:S(2)}) collective-permute-start(bf16[512,1024]{1,0:T(8,128)(2,1)} %pad_maximum_fusion.7), channel_id=1, source_target_pairs={{0,2},{2,0},{4,6},{6,4},{8,10},{10,8},{12,14},{14,12},{1,3},{3,1},... | collective-permute-start | bytes 3145736 | tf_op jit(solution)/shard_map/ppermute | solution.py:683
  110.5 42.5 %collective-permute-start.9 = (bf16[1024,512]{1,0:T(8,128)(2,1)}, bf16[1024,512]{1,0:T(8,128)(2,1)S(1)}, u32[]{:S(2)}, u32[]{:S(2)}) collective-permute-start(bf16[1024,512]{1,0:T(8,128)(2,1)} %collective-permute-done.8), channel_id=1, source_target_pairs={{4,0},{6,2},{8,12},{10,14},{5,1},{7,3},{9,13},{11,15},{20,16},{22,... | collective-permute-start | bytes 3145736 | tf_op jit(solution)/shard_map/ppermute | solution.py:683
  114.7 43.7 %collective-permute-start.7 = (bf16[512,1024]{1,0:T(8,128)(2,1)S(1)}, bf16[512,1024]{1,0:T(8,128)(2,1)S(1)}, u32[]{:S(2)}, u32[]{:S(2)}) collective-permute-start(bf16[512,1024]{1,0:T(8,128)(2,1)S(1)} %get-tuple-element.124), channel_id=1, source_target_pairs={{0,2},{2,0},{4,6},{6,4},{8,10},{10,8},{12,14},{14,12},{1,3},{3,1},... | collective-permute-start | bytes 3145736 | tf_op jit(solution)/shard_map/ppermute | solution.py:683
  130.6 53.2 %collective-permute-start.15 = (bf16[384,2048]{1,0:T(8,128)(2,1)}, bf16[384,2048]{1,0:T(8,128)(2,1)}, u32[]{:S(2)}, u32[]{:S(2)}) collective-permute-start(bf16[384,2048]{1,0:T(8,128)(2,1)} %get-tuple-element.136), channel_id=1, source_target_pairs={{0,4},{2,6},{4,0},{6,2},{8,12},{10,14},{12,8},{14,10},{1,5},{3,7},... | collective-permute-start | bytes 4718600 | tf_op jit(solution)/shard_map/ppermute | solution.py:683
  136.4 87.7 %collective-permute-start.18 = (bf16[2048,512]{1,0:T(8,128)(2,1)}, bf16[2048,512]{1,0:T(8,128)(2,1)}, u32[]{:S(2)}, u32[]{:S(2)}) collective-permute-start(bf16[2048,512]{1,0:T(8,128)(2,1)} %pad_maximum_fusion.5), channel_id=1, source_target_pairs={{4,8},{6,10},{8,4},{10,6},{5,9},{7,11},{9,5},{11,7},{20,24},{22,26... | collective-permute-start | bytes 6291464 | tf_op jit(solution)/shard_map/ppermute | solution.py:683
  152.9 62.1 %collective-permute-start.13 = (bf16[256,2048]{1,0:T(8,128)(2,1)}, bf16[256,2048]{1,0:T(8,128)(2,1)}, u32[]{:S(2)}, u32[]{:S(2)}) collective-permute-start(bf16[256,2048]{1,0:T(8,128)(2,1)} %get-tuple-element.133), channel_id=1, source_target_pairs={{0,4},{2,6},{12,8},{14,10},{1,5},{3,7},{13,9},{15,11},{16,20},{18,... | collective-permute-start | bytes 3145736 | tf_op jit(solution)/shard_map/ppermute | solution.py:683
  158.3 54.7 %collective-permute-start.11 = (bf16[1024,512]{1,0:T(8,128)(2,1)}, bf16[1024,512]{1,0:T(8,128)(2,1)}, u32[]{:S(2)}, u32[]{:S(2)}) collective-permute-start(bf16[1024,512]{1,0:T(8,128)(2,1)} %get-tuple-element.129), channel_id=1, source_target_pairs={{0,2},{2,0},{4,6},{6,4},{8,10},{10,8},{12,14},{14,12},{1,3},{3,1},... | collective-permute-start | bytes 3145736 | tf_op jit(solution)/shard_map/ppermute | solution.py:683
  187.2 236.3 %all-gather.17.cloned.1.call-start = ((), (), s32[]{:S(2)}) async-start(), calls=%async_computation.1 | async-start | bytes 9437184 | tf_op jit(solution)/shard_map/all_gather | solution.py:928
  224.2 48.2 %collective-permute-start.19 = (bf16[2048,512]{1,0:T(8,128)(2,1)}, bf16[2048,512]{1,0:T(8,128)(2,1)S(1)}, u32[]{:S(2)}, u32[]{:S(2)}) collective-permute-start(bf16[2048,512]{1,0:T(8,128)(2,1)} %pad_maximum_fusion.4), channel_id=1, source_target_pairs={{0,2},{2,0},{4,6},{6,4},{8,10},{10,8},{12,14},{14,12},{1,3},{3,1},... | collective-permute-start | bytes 6291464 | tf_op jit(solution)/shard_map/ppermute | solution.py:683
  225.6 85.7 %collective-permute-start.24 = (bf16[2048,512]{1,0:T(8,128)(2,1)}, bf16[2048,512]{1,0:T(8,128)(2,1)}, u32[]{:S(2)}, u32[]{:S(2)}) collective-permute-start(bf16[2048,512]{1,0:T(8,128)(2,1)} %collective-permute-done.18), channel_id=1, source_target_pairs={{4,0},{6,2},{8,12},{10,14},{5,1},{7,3},{9,13},{11,15},{20,16},{22,... | collective-permute-start | bytes 6291464 | tf_op jit(solution)/shard_map/ppermute | solution.py:683
  226.9 84.4 %collective-permute-start.22 = (bf16[2048,512]{1,0:T(8,128)(2,1)}, bf16[2048,512]{1,0:T(8,128)(2,1)}, u32[]{:S(2)}, u32[]{:S(2)}) collective-permute-start(bf16[2048,512]{1,0:T(8,128)(2,1)} %pad_maximum_fusion.4), channel_id=1, source_target_pairs={{4,8},{6,10},{8,4},{10,6},{5,9},{7,11},{9,5},{11,7},{20,24},{22,26... | collective-permute-start | bytes 6291464 | tf_op jit(solution)/shard_map/ppermute | solution.py:683
  232.8 76.3 %collective-permute-start.17 = (bf16[384,2048]{1,0:T(8,128)(2,1)S(1)}, bf16[384,2048]{1,0:T(8,128)(2,1)S(1)}, u32[]{:S(2)}, u32[]{:S(2)}) collective-permute-start(bf16[384,2048]{1,0:T(8,128)(2,1)S(1)} %get-tuple-element.138), channel_id=1, source_target_pairs={{0,4},{2,6},{4,0},{6,2},{8,12},{10,14},{12,8},{14,10},{1,5},{3,7},... | collective-permute-start | bytes 4718600 | tf_op jit(solution)/shard_map/ppermute | solution.py:683
  272.4 48.8 %collective-permute-start.20 = (bf16[512,2048]{1,0:T(8,128)(2,1)}, bf16[512,2048]{1,0:T(8,128)(2,1)}, u32[]{:S(2)}, u32[]{:S(2)}) collective-permute-start(bf16[512,2048]{1,0:T(8,128)(2,1)} %pad_maximum_fusion.3), channel_id=1, source_target_pairs={{0,2},{2,0},{4,6},{6,4},{8,10},{10,8},{12,14},{14,12},{1,3},{3,1},... | collective-permute-start | bytes 6291464 | tf_op jit(solution)/shard_map/ppermute | solution.py:683
  311.3 389.6 %all-gather.27.cloned.1.call-start = ((), (), s32[]{:S(2)}) async-start(), calls=%async_computation.7 | async-start | bytes 3145728 | tf_op jit(solution)/shard_map/all_gather | solution.py:1110
  316.3 48.7 %collective-permute-start.25 = (bf16[2048,512]{1,0:T(8,128)(2,1)}, bf16[2048,512]{1,0:T(8,128)(2,1)}, u32[]{:S(2)}, u32[]{:S(2)}) collective-permute-start(bf16[2048,512]{1,0:T(8,128)(2,1)} %get-tuple-element.146), channel_id=1, source_target_pairs={{0,2},{2,0},{4,6},{6,4},{8,10},{10,8},{12,14},{14,12},{1,3},{3,1},... | collective-permute-start | bytes 6291464 | tf_op jit(solution)/shard_map/ppermute | solution.py:683
  316.9 51.2 %collective-permute-start.23 = (bf16[512,2048]{1,0:T(8,128)(2,1)}, bf16[512,2048]{1,0:T(8,128)(2,1)}, u32[]{:S(2)}, u32[]{:S(2)}) collective-permute-start(bf16[512,2048]{1,0:T(8,128)(2,1)} %collective-permute-done.16), channel_id=1, source_target_pairs={{4,0},{6,2},{8,12},{10,14},{5,1},{7,3},{9,13},{11,15},{20,16},{22,... | collective-permute-start | bytes 6291464 | tf_op jit(solution)/shard_map/ppermute | solution.py:683
  321.3 46.9 %collective-permute-start.21 = (bf16[512,2048]{1,0:T(8,128)(2,1)}, bf16[512,2048]{1,0:T(8,128)(2,1)}, u32[]{:S(2)}, u32[]{:S(2)}) collective-permute-start(bf16[512,2048]{1,0:T(8,128)(2,1)} %pad_maximum_fusion.3), channel_id=1, source_target_pairs={{4,8},{6,10},{8,4},{10,6},{5,9},{7,11},{9,5},{11,7},{20,24},{22,26... | collective-permute-start | bytes 6291464 | tf_op jit(solution)/shard_map/ppermute | solution.py:683
  373.6 46.8 %collective-permute-start.26 = (bf16[512,2048]{1,0:T(8,128)(2,1)}, bf16[512,2048]{1,0:T(8,128)(2,1)}, u32[]{:S(2)}, u32[]{:S(2)}) collective-permute-start(bf16[512,2048]{1,0:T(8,128)(2,1)} %get-tuple-element.147), channel_id=1, source_target_pairs={{0,2},{2,0},{4,6},{6,4},{8,10},{10,8},{12,14},{14,12},{1,3},{3,1},... | collective-permute-start | bytes 6291464 | tf_op jit(solution)/shard_map/ppermute | solution.py:683
  458.2 45.6 %collective-permute-start.51 = (bf16[2048,512]{1,0:T(8,128)(2,1)S(1)}, bf16[2048,512]{1,0:T(8,128)(2,1)S(1)}, u32[]{:S(2)}, u32[]{:S(2)}) collective-permute-start(bf16[2048,512]{1,0:T(8,128)(2,1)S(1)} %convolution_convert_fusion.7), channel_id=1, source_target_pairs={{0,2},{2,0},{4,6},{6,4},{8,10},{10,8},{12,14},{14,12},{1,3},{3,1},... | collective-permute-start | bytes 6291464 | tf_op jit(solution)/shard_map/ppermute | solution.py:683
  509.8 44.2 %collective-permute-start.54 = (bf16[2048,512]{1,0:T(8,128)(2,1)}, bf16[2048,512]{1,0:T(8,128)(2,1)}, u32[]{:S(2)}, u32[]{:S(2)}) collective-permute-start(bf16[2048,512]{1,0:T(8,128)(2,1)} %add_convert_fusion), channel_id=1, source_target_pairs={{0,4},{2,6},{12,8},{14,10},{1,5},{3,7},{13,9},{15,11},{16,20},{18,... | collective-permute-start | bytes 6291464 | tf_op jit(solution)/shard_map/ppermute | solution.py:683
  527.3 43.5 %collective-permute-start.44 = (bf16[512,2048]{1,0:T(8,128)(2,1)S(1)}, bf16[512,2048]{1,0:T(8,128)(2,1)S(1)}, u32[]{:S(2)}, u32[]{:S(2)}) collective-permute-start(bf16[512,2048]{1,0:T(8,128)(2,1)S(1)} %convolution_convert_fusion.5), channel_id=1, source_target_pairs={{0,2},{2,0},{4,6},{6,4},{8,10},{10,8},{12,14},{14,12},{1,3},{3,1},... | collective-permute-start | bytes 6291464 | tf_op jit(solution)/shard_map/ppermute | solution.py:683
  576.7 48.1 %collective-permute-start.47 = (bf16[512,2048]{1,0:T(8,128)(2,1)}, bf16[512,2048]{1,0:T(8,128)(2,1)}, u32[]{:S(2)}, u32[]{:S(2)}) collective-permute-start(bf16[512,2048]{1,0:T(8,128)(2,1)} %add_convert_fusion.1), channel_id=1, source_target_pairs={{0,4},{2,6},{12,8},{14,10},{1,5},{3,7},{13,9},{15,11},{16,20},{18,... | collective-permute-start | bytes 6291464 | tf_op jit(solution)/shard_map/ppermute | solution.py:683
  579.3 47.8 %collective-permute-start.50 = (bf16[2048,512]{1,0:T(8,128)(2,1)}, bf16[2048,512]{1,0:T(8,128)(2,1)}, u32[]{:S(2)}, u32[]{:S(2)}) collective-permute-start(bf16[2048,512]{1,0:T(8,128)(2,1)} %convolution_convert_fusion.6), channel_id=1, source_target_pairs={{0,2},{2,0},{4,6},{6,4},{8,10},{10,8},{12,14},{14,12},{1,3},{3,1},... | collective-permute-start | bytes 6291464 | tf_op jit(solution)/shard_map/ppermute | solution.py:683
  580.8 46.3 %collective-permute-start.52 = (bf16[2048,512]{1,0:T(8,128)(2,1)}, bf16[2048,512]{1,0:T(8,128)(2,1)}, u32[]{:S(2)}, u32[]{:S(2)}) collective-permute-start(bf16[2048,512]{1,0:T(8,128)(2,1)} %add_convert_fusion), channel_id=1, source_target_pairs={{4,8},{6,10},{8,4},{10,6},{5,9},{7,11},{9,5},{11,7},{20,24},{22,26... | collective-permute-start | bytes 6291464 | tf_op jit(solution)/shard_map/ppermute | solution.py:683
  584.3 47.0 %collective-permute-start.56 = (bf16[2048,256]{1,0:T(8,128)(2,1)S(1)}, bf16[2048,256]{1,0:T(8,128)(2,1)S(1)}, u32[]{:S(2)}, u32[]{:S(2)}) collective-permute-start(bf16[2048,256]{1,0:T(8,128)(2,1)S(1)} %slice.385), channel_id=1, source_target_pairs={{4,0},{6,2},{8,12},{10,14},{5,1},{7,3},{9,13},{11,15},{20,16},{22,... | collective-permute-start | bytes 3145736 | tf_op jit(solution)/shard_map/ppermute | solution.py:683
  600.4 71.6 %collective-permute-start.28 = (bf16[384,2048]{1,0:T(8,128)(2,1)}, bf16[384,2048]{1,0:T(8,128)(2,1)}, u32[]{:S(2)}, u32[]{:S(2)}) collective-permute-start(bf16[384,2048]{1,0:T(8,128)(2,1)} %add_convert_fusion.2), channel_id=1, source_target_pairs={{0,4},{2,6},{4,0},{6,2},{8,12},{10,14},{12,8},{14,10},{1,5},{3,7},... | collective-permute-start | bytes 4718600 | tf_op jit(solution)/shard_map/ppermute | solution.py:731
  624.9 76.1 %collective-permute-start.48 = (bf16[512,2048]{1,0:T(8,128)(2,1)}, bf16[512,2048]{1,0:T(8,128)(2,1)}, u32[]{:S(2)}, u32[]{:S(2)}) collective-permute-start(bf16[512,2048]{1,0:T(8,128)(2,1)} %collective-permute-done.47), channel_id=1, source_target_pairs={{4,8},{6,10},{8,4},{10,6},{5,9},{7,11},{9,5},{11,7},{20,24},{22,26... | collective-permute-start | bytes 6291464 | tf_op jit(solution)/shard_map/ppermute | solution.py:683
  644.0 106.3 %all-gather.29.cloned.1.call-start = ((), (), s32[]{:S(2)}) async-start(), calls=%async_computation.8 | async-start | bytes 3145728 | tf_op jit(solution)/shard_map/all_gather | solution.py:1110
  651.1 39.6 %collective-permute-start.53 = (bf16[2048,256]{1,0:T(8,128)(2,1)}, bf16[2048,256]{1,0:T(8,128)(2,1)}, u32[]{:S(2)}, u32[]{:S(2)}) collective-permute-start(bf16[2048,256]{1,0:T(8,128)(2,1)} %fusion.9), channel_id=1, source_target_pairs={{0,4},{2,6},{4,0},{6,2},{8,12},{10,14},{12,8},{14,10},{1,5},{3,7},... | collective-permute-start | bytes 3145736 | tf_op jit(solution)/shard_map/ppermute | solution.py:683
  687.0 47.4 %collective-permute-start.43 = (bf16[512,2048]{1,0:T(8,128)(2,1)}, bf16[512,2048]{1,0:T(8,128)(2,1)}, u32[]{:S(2)}, u32[]{:S(2)}) collective-permute-start(bf16[512,2048]{1,0:T(8,128)(2,1)} %convolution_convert_fusion.4), channel_id=1, source_target_pairs={{0,2},{2,0},{4,6},{6,4},{8,10},{10,8},{12,14},{14,12},{1,3},{3,1},... | collective-permute-start | bytes 6291464 | tf_op jit(solution)/shard_map/ppermute | solution.py:683
  688.6 45.9 %collective-permute-start.45 = (bf16[512,2048]{1,0:T(8,128)(2,1)}, bf16[512,2048]{1,0:T(8,128)(2,1)}, u32[]{:S(2)}, u32[]{:S(2)}) collective-permute-start(bf16[512,2048]{1,0:T(8,128)(2,1)} %add_convert_fusion.1), channel_id=1, source_target_pairs={{4,8},{6,10},{8,4},{10,6},{5,9},{7,11},{9,5},{11,7},{20,24},{22,26... | collective-permute-start | bytes 6291464 | tf_op jit(solution)/shard_map/ppermute | solution.py:683
  701.0 162.1 %all-gather.31.cloned.1.call-start = ((), (), s32[]{:S(2)}) async-start(), calls=%async_computation.9 | async-start | bytes 3145728 | tf_op jit(solution)/shard_map/all_gather | solution.py:1110
  750.3 196.5 %reduce-scatter.2.cloned.1.call-start = ((), (), s32[]{:S(2)}) async-start(), calls=%async_computation.3 | async-start | bytes 9437184 | tf_op jit(solution)/shard_map/reduce_scatter | solution.py:1042
  769.2 189.7 %all-gather.33.cloned.1.call-start = ((), (), s32[]{:S(2)}) async-start(), calls=%async_computation.10 | async-start | bytes 3145728 | tf_op jit(solution)/shard_map/all_gather | solution.py:1110
  804.3 70.4 %collective-permute-start.58 = (bf16[1024,512]{1,0:T(8,128)(2,1)}, bf16[1024,512]{1,0:T(8,128)(2,1)}, u32[]{:S(2)}, u32[]{:S(2)}) collective-permute-start(bf16[1024,512]{1,0:T(8,128)(2,1)} %convolution_convert_fusion.16), channel_id=1, source_target_pairs={{0,2},{2,0},{4,6},{6,4},{8,10},{10,8},{12,14},{14,12},{1,3},{3,1},... | collective-permute-start | bytes 3145736 | tf_op jit(solution)/shard_map/ppermute | solution.py:683
  863.1 221.8 %all-gather.23.cloned.1.call-start = ((), (), s32[]{:S(2)}) async-start(), calls=%async_computation.5 | async-start | bytes 4718592 | tf_op jit(solution)/shard_map/all_gather | solution.py:928
  888.3 203.7 %all-gather.35.cloned.1.call-start = ((), (), s32[]{:S(2)}) async-start(), calls=%async_computation.11 | async-start | bytes 1572864 | tf_op jit(solution)/shard_map/all_gather | solution.py:1110
  916.5 35.2 %collective-permute-start.61 = (bf16[1024,256]{1,0:T(8,128)(2,1)}, bf16[1024,256]{1,0:T(8,128)(2,1)}, u32[]{:S(2)}, u32[]{:S(2)}) collective-permute-start(bf16[1024,256]{1,0:T(8,128)(2,1)} %fusion.21), channel_id=1, source_target_pairs={{0,4},{2,6},{4,0},{6,2},{8,12},{10,14},{12,8},{14,10},{1,5},{3,7},... | collective-permute-start | bytes 1572872 | tf_op jit(solution)/shard_map/ppermute | solution.py:683
  949.5 56.1 %collective-permute-start.30 = (bf16[384,2048]{1,0:T(8,128)(2,1)}, bf16[384,2048]{1,0:T(8,128)(2,1)}, u32[]{:S(2)}, u32[]{:S(2)}) collective-permute-start(bf16[384,2048]{1,0:T(8,128)(2,1)} %slice.358), channel_id=1, source_target_pairs={{0,4},{2,6},{4,0},{6,2},{8,12},{10,14},{12,8},{14,10},{1,5},{3,7},... | collective-permute-start | bytes 4718600 | tf_op jit(solution)/shard_map/ppermute | solution.py:683
  959.0 136.4 %all-gather.21.cloned.1.call-start = ((), (), s32[]{:S(2)}) async-start(), calls=%async_computation.4 | async-start | bytes 4718592 | tf_op jit(solution)/shard_map/all_gather | solution.py:928
  967.9 50.9 %collective-permute-start.62 = (f32[8,267,128]{2,0,1:T(8,128)}, f32[8,267,128]{2,0,1:T(8,128)S(1)}, u32[]{:S(2)}, u32[]{:S(2)}) collective-permute-start(f32[8,267,128]{2,0,1:T(8,128)} %copy.107), channel_id=1, source_target_pairs={{0,1},{1,0},{2,3},{3,2},{4,5},{5,4},{6,7},{7,6},{8,9},{9,8},{10,11... | collective-permute-start | bytes 3280904 | tf_op jit(solution)/shard_map/ppermute | solution.py:728
  975.5 44.7 %collective-permute-start.38 = (bf16[512,1024]{1,0:T(8,128)(2,1)}, bf16[512,1024]{1,0:T(8,128)(2,1)}, u32[]{:S(2)}, u32[]{:S(2)}) collective-permute-start(bf16[512,1024]{1,0:T(8,128)(2,1)} %convolution_convert_fusion.14), channel_id=1, source_target_pairs={{0,2},{2,0},{4,6},{6,4},{8,10},{10,8},{12,14},{14,12},{1,3},{3,1},... | collective-permute-start | bytes 3145736 | tf_op jit(solution)/shard_map/ppermute | solution.py:683
  979.9 40.3 %collective-permute-start.41 = (bf16[512,1024]{1,0:T(8,128)(2,1)}, bf16[512,1024]{1,0:T(8,128)(2,1)}, u32[]{:S(2)}, u32[]{:S(2)}) collective-permute-start(bf16[512,1024]{1,0:T(8,128)(2,1)} %add.283), channel_id=1, source_target_pairs={{4,8},{6,10},{8,4},{10,6},{5,9},{7,11},{9,5},{11,7},{20,24},{22,26... | collective-permute-start | bytes 3145736 | tf_op jit(solution)/shard_map/ppermute | solution.py:683
  1039.7 35.7 %collective-permute-start.65 = (f32[1,267,128]{2,1,0:T(8,128)S(1)}, f32[1,267,128]{2,1,0:T(8,128)S(1)}, u32[]{:S(2)}, u32[]{:S(2)}) collective-permute-start(f32[1,267,128]{2,1,0:T(8,128)S(1)} %slice.406), channel_id=1, source_target_pairs={{0,4},{2,6},{4,0},{6,2},{8,12},{10,14},{12,8},{14,10},{1,5},{3,7},... | collective-permute-start | bytes 410120 | tf_op jit(solution)/shard_map/ppermute | solution.py:683
  (119 other events, 1922.8 us)
Sparse Core Ops, SparseCore 0:
  35.5 49.0 all-gather.24
  644.1 52.2 all-gather.26
  701.1 31.8 all-gather.28
  750.4 33.6 all-gather.30
  863.2 33.1 all-gather.32
  897.8 12.1 all-gather.22
  959.1 22.0 all-gather.34
  1010.2 12.4 all-gather.20
Sparse Core Ops, SparseCore 1:
  187.3 16.4 all-gather.18
  311.4 15.4 all-gather.16
  769.3 14.8 reduce-scatter.1
where the time goes:
time: 1120 us; the launch traced here: 1110 us
  waiting for transfers between devices  367 us (33%)
  starting transfers between devices  205 us (18%)
  Pallas kernels  180 us (16%)
  matrix products  178 us (16%)
  local copies, waits for them, and re-layouts  84.7 us (8%)
  other arithmetic  76.6 us (7%)
  between operations  17.7 us (2%)
    ppermute x54, waiting for transfers between devices, send(): arrived = lax.ppermute(block, axis, pairs)  356 us
    pallas_call x26, Pallas kernels, call(): pl.pallas_call(body, out_shape=out_shape, grid_spec=pltpu.PrefetchScalarG...  180 us
    dot_general x32, matrix products, mm(): return lax.dot_general(a, b, dims, preferred_element_type=f32)  178 us
    ppermute x54, starting transfers between devices, send(): arrived = lax.ppermute(block, axis, pairs)  167 us
    unnamed x194, local copies, waits for them, and re-layouts  54.8 us
    ppermute x1, starting transfers between devices, pair_now(): return lax.ppermute(block, 'dp', self.pair)  24.5 us
    unnamed x9, other arithmetic  22.8 us
  transfers between devices with their start and end apart: 79, of which 26 were waited for; matrix products, arithmetic and copies ran while one was open for 27% of the time, Pallas kernels for 14%

commit v1 on v0

--- a/solution.py
+++ b/solution.py
@@ -735,6 +735,18 @@
     return lax.optimization_barrier((value, *earlier))[0]
 
 
+class Order:
+    def __init__(self):
+        self.last = ()
+
+    def tie(self, value):
+        return after(value, *self.last) if self.last else value
+
+    def mark(self, *values):
+        self.last = values
+        return values[0]
+
+
 class Gathered:
     def __init__(self, links, axis, mine, other=None):
         self.links, self.axis, self.mine, self.other = links, axis, mine, other
@@ -778,42 +790,47 @@
 
 
 class Reduced:
-    def __init__(self, links, axis, size, halved, part):
-        self.links, self.axis, self.size, self.halved, self.part = links, axis, size, halved, part
+    def __init__(self, links, order, axis, size, halved, part):
+        self.links, self.order, self.axis, self.size = links, order, axis, size
+        self.halved, self.part = halved, part
         self.landed = {}
 
     def pair_sum(self, o):
         total = self.part(o, 2)
         for block in self.landed.pop(o, []):
             total = total + block.astype(f32)
-        return total.astype(bf16)
+        return self.order.mark(total.astype(bf16))
 
     def one(self, block, o):
         return lax.slice_in_dim(
             block, o * self.size, (o + 1) * self.size, axis=self.axis
         ).astype(f32)
 
-    def far(self):
-        sent = []
+    def far(self, level, o):
+        arrived = self.links.to_far(self.pair_sum(o), level)
+        self.landed.setdefault(o - (1 << level), []).append(arrived)
+        return arrived
+
+    def far_rest(self, done):
+        arrived = None
         for level in range(self.links.levels - 1, 1, -1):
             for o in reversed(range(1 << level, 2 << level, 2)):
-                sent.append(self.pair_sum(o))
-                arrived = self.links.to_far(sent[-1], level)
-                self.landed.setdefault(o - (1 << level), []).append(arrived)
-        return sent
+                if (level, o) not in done:
+                    arrived = self.far(level, o)
+        return arrived
 
     def inward(self):
         self.ahead = self.pair_sum(2)
         self.passed = self.links.to_side(self.ahead, self.links.inward)
-        return self.ahead
+        if self.halved:
+            self.direct = self.links.to_middle(self.ahead)
 
     def middle(self):
-        self.direct = self.links.to_middle(
-            self.ahead if self.halved else self.ahead + self.passed
-        )
-
-    def middle_rest(self):
-        self.relay = self.links.to_middle(self.passed)
+        if self.halved:
+            self.relay = self.links.to_middle(self.order.tie(self.passed))
+        else:
+            both = self.order.mark(self.order.tie(self.ahead) + self.passed)
+            self.direct = self.links.to_middle(both)
 
     def single(self, o):
         total = self.part(o, 1)
@@ -822,18 +839,18 @@
         return total
 
     def near(self):
-        value = self.single(1).astype(bf16)
+        value = self.order.mark(self.single(1).astype(bf16))
         self.theirs = self.links.to_side(value, self.links.pair).astype(f32)
-        return value
 
     def outward(self):
-        value = self.one(self.relay, 1).astype(bf16)
+        value = self.one(self.order.tie(self.relay), 1).astype(bf16)
         self.last = self.links.to_side(value, self.links.outward).astype(f32)
 
     def result(self):
         if not self.halved:
-            return self.single(0) + self.theirs, None
-        return self.single(0) + self.last, self.theirs + self.one(self.relay, 0)
+            return self.order.mark(self.single(0) + self.theirs), None
+        own = self.order.mark(self.single(0) + self.last)
+        return own, self.theirs + self.one(self.relay, 0)
 
 
 def local(
@@ -984,82 +1001,67 @@
     acts, grad_pre, grad_bias_up = hidden_units(normed_all, w_up, bias_up[None], hidden_grad)
 
     links.wire.window = 1 << 30
+    order = Order()
+    tie, mark = order.tie, order.mark
     sum_down = Reduced(
-        links, 1, part, True, lambda o, b: mm(acts, block(cot_all, o, b), tn)
+        links, order, 1, part, True, lambda o, b: mm(tie(acts), block(cot_all, o, b), tn)
     )
     sum_up = Reduced(
-        links, 0, part, True, lambda o, b: mm(block(normed_all, o, b), grad_pre, tn)
-    )
-    sent_down = sum_down.far()
-    w_up_late = after(w_up, *sent_down)
+        links, order, 0, part, True, lambda o, b: mm(block(normed_all, o, b), tie(grad_pre), tn)
+    )
+    early = [(2, 6)] if levels == 3 else []
+    for level, o in early:
+        sum_down.far(level, o)
     pre_give = lax.dynamic_slice_in_dim(grad_pre, (1 - split) * 2 * mine, 2 * mine)
     pre_keep = lax.dynamic_slice_in_dim(grad_pre, split * 2 * mine, 2 * mine)
-    two_give = mm(pre_give, w_up_late, nt).astype(bf16)
+    two_give = mark(mm(pre_give, tie(w_up), nt).astype(bf16))
     two_other = across(two_give)
-    two_keep = mm(pre_keep, after(w_up_late, two_give), nt).astype(bf16)
+    down_landed = sum_down.far_rest(early)
+    two_keep = mark(mm(pre_keep, tie(w_up), nt).astype(bf16))
     two_theirs = two_keep[mine:].astype(f32) + two_other[mine:].astype(f32)
-    two_pair = links.pair_now(swap_small(two_theirs.astype(bf16), part))
-    sent_up = sum_up.far()
+    two_theirs = mark(swap_small(two_theirs.astype(bf16), part))
+    two_pair = links.pair_now(two_theirs)
+    up_landed = sum_up.far_rest([])
     sum_down.inward()
-    sum_down.middle()
     dh, dh_mine, grad_gain_two, grad_bias_two, grad_bias_out = middle_backward(
-        middle, two_keep, two_other, two_pair, cot_own, gain_two, part
-    )
+        middle, tie(two_keep), two_other, two_pair, cot_own, gain_two, part
+    )
+    mark(dh_mine)
     dh_low = jnp.concatenate([dh_mine, across(dh_mine)], axis=0)
-
-    grad_att = mm(dh_low, after(w_attn, *sent_up), nt).astype(bf16)
+    grad_att = mark(mm(dh_low, w_attn, nt).astype(bf16))
     dots = jnp.sum(
         (grad_att.astype(f32) * attended.astype(f32)).reshape(total, heads, HD), axis=2
     )
     grad_queries, kv_part = attention_backward(
-        queries, grad_att, key_value, limits_t, log_totals.T[:heads], dots.T, heads
-    )
-    sum_down.middle_rest()
+        queries, after(grad_att, down_landed), key_value, limits_t, log_totals.T[:heads], dots.T,
+        heads,
+    )
+    mark(grad_queries)
+    sum_down.middle()
+    one_give = mark(mm(grad_queries[mine:], w_query, nt).astype(bf16))
+    one_other = across(one_give)
+    kv_other = across(kv_part[mine:])
     sum_down.near()
+    sum_up.inward()
+    sum_attn = Reduced(
+        links, order, 1, part, False, lambda o, b: mm(tie(attended), block(dh_low, o, b), tn)
+    )
+    sum_attn.far_rest([])
+    one_keep = mark(mm(grad_queries[:mine], tie(w_query), nt).astype(bf16))
+    kv_low = (kv_part[:mine] + kv_other).astype(bf16)
+    grad_mine, grad_gain_one, grad_bias_one = first_backward(
+        x_rel, after(one_keep, up_landed), one_other, kv_low, w_keyval_t, dh, gain_one, ids, count
+    )
+    mark(grad_mine)
+    tokens_grad = both_rows(grad_mine)
+    sum_query = Reduced(
+        links, order, 0, part, False, lambda o, b: mm(block(normed, o, b), tie(grad_queries), tn)
+    )
+    sum_query.far_rest([])
+    sum_up.middle()
     sum_down.outward()
-    sum_attn = Reduced(
-        links, 1, part, False, lambda o, b: mm(attended, block(dh_low, o, b), tn)
-    )
-    sent_attn = sum_attn.far()
-    one_give = mm(grad_queries[mine:], w_query, nt).astype(bf16)
-    one_other = across(one_give)
-    one_keep = mm(grad_queries[:mine], w_query, nt).astype(bf16)
-    kv_low = (kv_part[:mine] + across(kv_part[mine:])).astype(bf16)
-    grad_keyval_t = mm(kv_low, normed[:mine], tn)
-    sum_up.inward()
-    sum_up.middle()
-    sum_query = Reduced(
-        links, 0, part, False, lambda o, b: mm(block(normed, o, b), grad_queries, tn)
-    )
-    sum_query.far()
-    sum_up.middle_rest()
-    grad_mine, grad_gain_one, grad_bias_one = first_backward(
-        x_rel, one_keep, one_other, kv_low, w_keyval_t, dh, gain_one, ids, count
-    )
-    tokens_grad = both_rows(grad_mine)
-
-    down_part = mm(after(acts, *sent_attn), w_down).astype(bf16)
-    down_sum = lax.psum_scatter(down_part, "tensor", scatter_dimension=0, tiled=True)
-
-    peers = across(after(tops, *sent_up))
-    peak = jnp.where(
-        split == 0, jnp.concatenate([tops, peers]), jnp.concatenate([peers, tops])
-    )
-    peak = jnp.maximum(peak, lax.ppermute(peak, "group", swap_group))
-    for pairs in [links.pair, links.mirror] + links.beside:
-        peak = jnp.maximum(peak, lax.ppermute(peak, "dp", pairs))
-    clip_rows = clip_limit / jnp.maximum(peak, clip_limit)
-
-    sum_up.near()
-    sum_up.outward()
-    sum_attn.inward()
-    sum_attn.middle()
-    sum_query.inward()
-    down_pair = links.to_pair(swap_small(down_sum[mine:], part))
-    block_out = both_rows(
-        block_result(middle, down_sum, down_pair, bias_down, ids, count)
-    )
-
+
+    grad_keyval_t = mm(tie(kv_low), normed[:mine], tn)
     grad_bias_query = jnp.sum(grad_queries.astype(f32), axis=0)
     spread = jnp.concatenate(
         [
@@ -1085,15 +1087,46 @@
         b = pick_blocks(spread, mirrored * splits + core, own_cols, count, True)
         return jnp.concatenate([a[:, : vec + 4], b[:, :1], a[:, vec + 4 :], b[:, 1:]], axis=1)
 
-    red_shared = pieces(split) + across(pieces(1 - split))
+    shared_give = mark(pieces(1 - split))
+    shared_other = across(shared_give)
+    red_down = sum_down.result()
+
+    down_part = mark(mm(tie(acts), w_down).astype(bf16))
+    down_sum = lax.psum_scatter(down_part, "tensor", scatter_dimension=0, tiled=True)
+    sum_up.near()
+    sum_attn.inward()
+
+    red_shared = pieces(split) + shared_other
+    keep = red_shared.shape[0] // 2
+    cube = list(reversed([links.pair, links.mirror] + links.beside))
+    for pairs in cube[:-2]:
+        keep = red_shared.shape[0] // 2
+        red_shared = red_shared[:keep] + lax.ppermute(red_shared[keep:], "dp", pairs)
+    sum_query.inward()
+    sum_attn.middle()
+    sum_up.outward()
+    down_pair = links.to_pair(swap_small(tie(down_sum)[mine:], part))
+
+    peers = across(tie(tops))
+    peak = jnp.where(
+        split == 0, jnp.concatenate([tops, peers]), jnp.concatenate([peers, tops])
+    )
+    peak = jnp.maximum(peak, lax.ppermute(peak, "group", swap_group))
+    for pairs in [links.pair, links.mirror] + links.beside:
+        peak = jnp.maximum(peak, lax.ppermute(peak, "dp", pairs))
+    clip_rows = clip_limit / jnp.maximum(peak, clip_limit)
+
     sum_query.middle()
+    red_up = sum_up.result()
     sum_attn.near()
-    for pairs in reversed([links.pair, links.mirror] + links.beside):
+    for pairs in cube[-2:]:
         keep = red_shared.shape[0] // 2
-        red_shared = red_shared[:keep] + links.to_side(red_shared[keep:], pairs)
+        red_shared = red_shared[:keep] + lax.ppermute(red_shared[keep:], "dp", pairs)
     red_shared = red_shared[0]
+    block_out = both_rows(
+        block_result(middle, down_sum, down_pair, bias_down, ids, count)
+    )
     sum_query.near()
-    red_down, red_up = sum_down.result(), sum_up.result()
     red_attn, red_query = sum_attn.result()[0], sum_query.result()[0]
 
     one_in, two_in = tall(first_in), tall(second_in)

time: 1120 us -> 1080 us (0.964)
  starting transfers between devices: 205 us -> 138 us
  waiting for transfers between devices: 367 us -> 400 us
    ppermute x54 -> x51, starting transfers between devices: 167 us -> 119 us  [send(): arrived = lax.ppermute(block, axis, pairs)]
    ppermute x1, starting transfers between devices: 24.5 us -> 2.01 us  [pair_now(): return lax.ppermute(block, 'dp', self.pair)]
    ppermute x54 -> x51, waiting for transfers between devices: 356 us -> 375 us  [send(): arrived = lax.ppermute(block, axis, pairs)]
    unnamed x194 -> x180, local copies, waits for them, and re-layouts: 54.8 us -> 50 us
    unnamed x9 -> x11, other arithmetic: 22.8 us -> 22.8 us
  transfers between devices with their start and end apart: 79 -> 79, of which waited for: 26 -> 31; matrix products, arithmetic and copies ran while one was open for 27% -> 27% of each run, Pallas kernels for 14% -> 14%
where the time goes in v1:
time: 1080 us; the launch traced here: 1070 us
  waiting for transfers between devices  400 us (37%)
  Pallas kernels  180 us (17%)
  matrix products  178 us (16%)
  starting transfers between devices  138 us (13%)
  local copies, waits for them, and re-layouts  80 us (7%)
  other arithmetic  76.8 us (7%)
  between operations  17.6 us (2%)
    ppermute x51, waiting for transfers between devices, send(): arrived = lax.ppermute(block, axis, pairs)  375 us
    pallas_call x26, Pallas kernels, call(): pl.pallas_call(body, out_shape=out_shape, grid_spec=pltpu.PrefetchScalarG...  180 us
    dot_general x32, matrix products, mm(): return lax.dot_general(a, b, dims, preferred_element_type=f32)  178 us
    ppermute x51, starting transfers between devices, send(): arrived = lax.ppermute(block, axis, pairs)  119 us
    unnamed x180, local copies, waits for them, and re-layouts  50 us
    unnamed x11, other arithmetic  22.8 us
  transfers between devices with their start and end apart: 79, of which 31 were waited for; matrix products, arithmetic and copies ran while one was open for 27% of the time, Pallas kernels for 14%

profile of v1, /device:TPU:0, one launch (start us, length us, event | category | flops | bytes accessed | tf_op | source)
XLA Modules:
  0.0 1070.6 jit_solution(8244939165408415536)
XLA Ops:
  18.7 8.7 collective-permute-done
  39.9 23.6 %collective-permute-done.2 = bf16[2048,256]{1,0:T(8,128)(2,1)} collective-permute-done((bf16[2048,256]{1,0:T(8,128)(2,1)}, bf16[2048,256]{1,0:T(8,128)(2,1)}, u32[]{:S(2)}, u32[]{:S(2)}) %collective-permute-start.2) | collective-permute-done | bytes 1048608 | tf_op jit(solution)/shard_map/ppermute | solution.py:683
  70.2 13.6 %collective-permute-done.5 = bf16[1024,256]{1,0:T(8,128)(2,1)} collective-permute-done((bf16[1024,256]{1,0:T(8,128)(2,1)}, bf16[1024,256]{1,0:T(8,128)(2,1)}, u32[]{:S(2)}, u32[]{:S(2)}) %collective-permute-start.5) | collective-permute-done | bytes 524320 | tf_op jit(solution)/shard_map/ppermute | solution.py:683
  92.5 11.6 %collective-permute-done.3 = bf16[512,1024]{1,0:T(8,128)(2,1)} collective-permute-done((bf16[512,1024]{1,0:T(8,128)(2,1)}, bf16[512,1024]{1,0:T(8,128)(2,1)}, u32[]{:S(2)}, u32[]{:S(2)}) %collective-permute-start.3) | collective-permute-done | bytes 1048608 | tf_op jit(solution)/shard_map/ppermute | solution.py:683
  118.1 12.5 %collective-permute-done.14 = bf16[256,2048]{1,0:T(8,128)(2,1)} collective-permute-done((bf16[256,2048]{1,0:T(8,128)(2,1)}, bf16[256,2048]{1,0:T(8,128)(2,1)}, u32[]{:S(2)}, u32[]{:S(2)}) %collective-permute-start.14) | collective-permute-done | bytes 1048608 | tf_op jit(solution)/shard_map/ppermute | solution.py:683
  140.7 12.3 %collective-permute-done.9 = bf16[1024,512]{1,0:T(8,128)(2,1)S(1)} collective-permute-done((bf16[1024,512]{1,0:T(8,128)(2,1)}, bf16[1024,512]{1,0:T(8,128)(2,1)S(1)}, u32[]{:S(2)}, u32[]{:S(2)}) %collective-permute-start.9) | collective-permute-done | bytes 1048608 | tf_op jit(solution)/shard_map/ppermute | solution.py:683
  173.9 9.9 collective-permute-done.15
  187.4 6.7 add_convert_fusion.3.q_ref
  196.8 16.2 %attention_forward.1 = (bf16[768,1024]{1,0:T(8,128)(2,1)S(1)}, f32[768,128]{1,0:T(8,128)S(1)}, f32[8,128]{1,0:T(8,128)S(1)}) custom-call(bf16[768,1024]{1,0:T(8,128)(2,1)S(1)} %add_convert_fusion.3.q_ref, bf16[768,256]{1,0:T(8,128)(2,1)S(1)} %convolution_convert_fusion.17.kv_ref, f32[768,768]{1,0:T(8,128)S(1)} %copy-done.19), custom_call_target="tpu_custom_call" | custom-call | flops 4831838208 | bytes 6295552 | tf_op jit(solution)/shard_map/attention_forward/pallas_call | solution.py:48
  232.9 34.3 %collective-permute-start.17 = (bf16[384,2048]{1,0:T(8,128)(2,1)S(1)}, bf16[384,2048]{1,0:T(8,128)(2,1)S(1)}, u32[]{:S(2)}, u32[]{:S(2)}) collective-permute-start(bf16[384,2048]{1,0:T(8,128)(2,1)S(1)} %get-tuple-element.168), channel_id=1, source_target_pairs={{0,4},{2,6},{4,0},{6,2},{8,12},{10,14},{12,8},{14,10},{1,5},{3,7},... | collective-permute-start | bytes 4718600 | tf_op jit(solution)/shard_map/ppermute | solution.py:683
  276.3 33.0 %collective-permute-done.17 = bf16[384,2048]{1,0:T(8,128)(2,1)S(1)} collective-permute-done((bf16[384,2048]{1,0:T(8,128)(2,1)S(1)}, bf16[384,2048]{1,0:T(8,128)(2,1)S(1)}, u32[]{:S(2)}, u32[]{:S(2)}) %collective-permute-start.17) | collective-permute-done | bytes 1572896 | tf_op jit(solution)/shard_map/ppermute | solution.py:683
  328.3 36.8 %collective-permute-done.25 = bf16[2048,512]{1,0:T(8,128)(2,1)} collective-permute-done((bf16[2048,512]{1,0:T(8,128)(2,1)}, bf16[2048,512]{1,0:T(8,128)(2,1)}, u32[]{:S(2)}, u32[]{:S(2)}) %collective-permute-start.25) | collective-permute-done | bytes 2097184 | tf_op jit(solution)/shard_map/ppermute | solution.py:683
  368.2 5.4 constant_dynamic-update-slice_fusion.12
  378.3 19.0 %convolution_convert_fusion.1.dz_ref = bf16[1536,2048]{1,0:T(8,128)(2,1)} fusion(bf16[1536,2048]{1,0:T(8,128)(2,1)} %all-gather.19.cloned.1.call-done, bf16[2048,2048]{1,0:T(8,128)(2,1)} %constant_dynamic-update-slice_fusion.15), kind=kOutput, calls=%fused_computation.1 | convolution fusion | flops 12888047616 | bytes 20971520 | tf_op jit(solution)/shard_map/dot_general | solution.py:939
  397.3 23.0 %collective-permute-done.26 = bf16[512,2048]{1,0:T(8,128)(2,1)S(1)} collective-permute-done((bf16[512,2048]{1,0:T(8,128)(2,1)}, bf16[512,2048]{1,0:T(8,128)(2,1)S(1)}, u32[]{:S(2)}, u32[]{:S(2)}) %collective-permute-start.26) | collective-permute-done | bytes 2097184 | tf_op jit(solution)/shard_map/ppermute | solution.py:683
  421.8 28.2 %hidden_units.1 = (bf16[1536,2048]{1,0:T(8,128)(2,1)S(1)}, bf16[1536,2048]{1,0:T(8,128)(2,1)S(1)}, f32[1,2048]{1,0:T(1,128)S(1)}) custom-call(bf16[1536,2048]{1,0:T(8,128)(2,1)} %all-gather.17.cloned.1.call-done.n_ref, bf16[2048,2048]{1,0:T(8,128)(2,1)} %constant_dynamic-update-slice_fusion.10.w_ref, f32[1,2048]{1,0:T(1,128)S(1)} %bitcast.191, ...), custom_call_target="tpu_custom_call" | custom-call | flops 12884901888 | bytes 33570816 | tf_op jit(solution)/shard_map/hidden_units/pallas_call | solution.py:48
  450.0 7.3 convolution_convert_fusion.7
  457.3 10.4 convolution_convert_fusion.3
  469.3 8.3 convolution_convert_fusion.6
  477.6 9.3 convolution_convert_fusion.2.a_ref
  500.4 15.8 %collective-permute-done.28 = bf16[2048,512]{1,0:T(8,128)(2,1)} collective-permute-done((bf16[2048,512]{1,0:T(8,128)(2,1)}, bf16[2048,512]{1,0:T(8,128)(2,1)}, u32[]{:S(2)}, u32[]{:S(2)}) %collective-permute-start.28) | collective-permute-done | bytes 2097184 | tf_op jit(solution)/shard_map/ppermute | solution.py:683
  516.1 6.4 add_convert_fusion.1
  550.8 30.4 %collective-permute-done.31 = bf16[2048,512]{1,0:T(8,128)(2,1)} collective-permute-done((bf16[2048,512]{1,0:T(8,128)(2,1)}, bf16[2048,512]{1,0:T(8,128)(2,1)}, u32[]{:S(2)}, u32[]{:S(2)}) %collective-permute-start.31) | collective-permute-done | bytes 2097184 | tf_op jit(solution)/shard_map/ppermute | solution.py:683
  591.7 26.3 %attention_backward.1 = (bf16[768,1024]{1,0:T(8,128)(2,1)S(1)}, f32[768,256]{1,0:T(8,128)S(1)}) custom-call(bf16[768,1024]{1,0:T(8,128)(2,1)S(1)} %copy-done.47, bf16[768,1024]{1,0:T(8,128)(2,1)S(1)} %copy-done.28, bf16[768,256]{1,0:T(8,128)(2,1)S(1)} %copy-done.44, f32[768,768]{1,0:T(8,128)S(1)} %copy-done.18, f32[8,768]{1,0:T(8,128)S(1)} %slice.359.lse_ref, ...), custom_call_target="tpu_custom_call" | custom-call | flops 12079595520 | bytes 8306688 | tf_op jit(solution)/shard_map/attention_backward/pallas_call | solution.py:48
  622.8 6.7 fusion.8
  632.0 38.7 %collective-permute-done.34 = bf16[512,2048]{1,0:T(8,128)(2,1)} collective-permute-done((bf16[512,2048]{1,0:T(8,128)(2,1)}, bf16[512,2048]{1,0:T(8,128)(2,1)}, u32[]{:S(2)}, u32[]{:S(2)}) %collective-permute-start.34) | collective-permute-done | bytes 2097184 | tf_op jit(solution)/shard_map/ppermute | solution.py:683
  670.7 6.4 add_convert_fusion
  734.6 7.3 fusion.6.g_ref
  741.9 7.2 adam_out.3
  749.1 18.8 %convolution_convert_fusion = bf16[1536,2048]{1,0:T(8,128)(2,1)} fusion(bf16[1536,2048]{1,0:T(8,128)(2,1)} %copy-done.45, bf16[2048,2048]{1,0:T(8,128)(2,1)} %constant_dynamic-update-slice_fusion.15), kind=kOutput, calls=%fused_computation | convolution fusion | flops 12888047616 | bytes 20971520 | tf_op jit(solution)/shard_map/dot_general | solution.py:939
  768.0 6.7 fusion.9
  784.8 7.2 adam_out.4
  798.3 6.4 collective-permute-done.43
  811.3 13.8 %collective-permute-done.50 = bf16[512,1024]{1,0:T(8,128)(2,1)} collective-permute-done((bf16[512,1024]{1,0:T(8,128)(2,1)}, bf16[512,1024]{1,0:T(8,128)(2,1)}, u32[]{:S(2)}, u32[]{:S(2)}) %collective-permute-start.50) | collective-permute-done | bytes 1048608 | tf_op jit(solution)/shard_map/ppermute | solution.py:683
  833.3 7.3 fusion.7.g_ref
  840.6 10.6 adam_in.3
  852.0 20.6 %collective-permute-done.60 = bf16[256,2048]{1,0:T(8,128)(2,1)} collective-permute-done((bf16[256,2048]{1,0:T(8,128)(2,1)}, bf16[256,2048]{1,0:T(8,128)(2,1)}, u32[]{:S(2)}, u32[]{:S(2)}) %collective-permute-start.60) | collective-permute-done | bytes 1048608 | tf_op jit(solution)/shard_map/ppermute | solution.py:683
  875.8 10.6 adam_in.4
  891.6 21.8 %collective-permute-done.54 = bf16[1024,512]{1,0:T(8,128)(2,1)S(1)} collective-permute-done((bf16[1024,512]{1,0:T(8,128)(2,1)}, bf16[1024,512]{1,0:T(8,128)(2,1)S(1)}, u32[]{:S(2)}, u32[]{:S(2)}) %collective-permute-start.54) | collective-permute-done | bytes 1048608 | tf_op jit(solution)/shard_map/ppermute | solution.py:683
  924.2 7.2 collective-permute-done.56
  947.0 14.3 %collective-permute-done.44.p_ref = bf16[384,2048]{1,0:T(8,128)(2,1)} collective-permute-done((bf16[384,2048]{1,0:T(8,128)(2,1)}, bf16[384,2048]{1,0:T(8,128)(2,1)}, u32[]{:S(2)}, u32[]{:S(2)}) %collective-permute-start.44) | collective-permute-done | bytes 1572896 | tf_op jit(solution)/shard_map/ppermute | solution.py:683
  970.6 5.3 collective-permute-done.64
  994.8 6.3 outer_out.3
  1007.3 6.2 outer_out.4
  1013.5 8.7 outer_in.3
  1022.1 8.7 outer_in.4
  1030.8 6.0 adam_in.5
  1039.0 7.2 collective-permute-done.66
  (451 shorter events, 383.9 us)
Async XLA Ops:
  8.0 153.9 %all-gather.25.cloned.1.call-start = ((), (), s32[]{:S(2)}) async-start(), calls=%async_computation.6 | async-start | bytes 2367488 | tf_op jit(solution)/shard_map/all_gather | solution.py:905
  35.4 342.9 %all-gather.19.cloned.1.call-start = ((), (), s32[]{:S(2)}) async-start(), calls=%async_computation.2 | async-start | bytes 9437184 | tf_op jit(solution)/shard_map/all_gather | solution.py:945
  37.7 46.0 %collective-permute-start.5 = (bf16[1024,256]{1,0:T(8,128)(2,1)}, bf16[1024,256]{1,0:T(8,128)(2,1)}, u32[]{:S(2)}, u32[]{:S(2)}) collective-permute-start(bf16[1024,256]{1,0:T(8,128)(2,1)} %get-tuple-element.378), channel_id=1, source_target_pairs={{0,4},{2,6},{4,0},{6,2},{8,12},{10,14},{12,8},{14,10},{1,5},{3,7},... | collective-permute-start | bytes 1572872 | tf_op jit(solution)/shard_map/ppermute | solution.py:683
  63.6 40.6 %collective-permute-start.3 = (bf16[512,1024]{1,0:T(8,128)(2,1)}, bf16[512,1024]{1,0:T(8,128)(2,1)}, u32[]{:S(2)}, u32[]{:S(2)}) collective-permute-start(bf16[512,1024]{1,0:T(8,128)(2,1)} %collective-permute-done.1), channel_id=1, source_target_pairs={{4,0},{6,2},{8,12},{10,14},{5,1},{7,3},{9,13},{11,15},{20,16},{22,... | collective-permute-start | bytes 3145736 | tf_op jit(solution)/shard_map/ppermute | solution.py:683
  68.7 40.3 %collective-permute-start.4 = (bf16[512,1024]{1,0:T(8,128)(2,1)}, bf16[512,1024]{1,0:T(8,128)(2,1)}, u32[]{:S(2)}, u32[]{:S(2)}) collective-permute-start(bf16[512,1024]{1,0:T(8,128)(2,1)} %pad_maximum_fusion.7), channel_id=1, source_target_pairs={{0,2},{2,0},{4,6},{6,4},{8,10},{10,8},{12,14},{14,12},{1,3},{3,1},... | collective-permute-start | bytes 3145736 | tf_op jit(solution)/shard_map/ppermute | solution.py:683
  110.5 42.5 %collective-permute-start.9 = (bf16[1024,512]{1,0:T(8,128)(2,1)}, bf16[1024,512]{1,0:T(8,128)(2,1)S(1)}, u32[]{:S(2)}, u32[]{:S(2)}) collective-permute-start(bf16[1024,512]{1,0:T(8,128)(2,1)} %collective-permute-done.8), channel_id=1, source_target_pairs={{4,0},{6,2},{8,12},{10,14},{5,1},{7,3},{9,13},{11,15},{20,16},{22,... | collective-permute-start | bytes 3145736 | tf_op jit(solution)/shard_map/ppermute | solution.py:683
  114.7 43.7 %collective-permute-start.7 = (bf16[512,1024]{1,0:T(8,128)(2,1)S(1)}, bf16[512,1024]{1,0:T(8,128)(2,1)S(1)}, u32[]{:S(2)}, u32[]{:S(2)}) collective-permute-start(bf16[512,1024]{1,0:T(8,128)(2,1)S(1)} %get-tuple-element.154), channel_id=1, source_target_pairs={{0,2},{2,0},{4,6},{6,4},{8,10},{10,8},{12,14},{14,12},{1,3},{3,1},... | collective-permute-start | bytes 3145736 | tf_op jit(solution)/shard_map/ppermute | solution.py:683
  130.6 53.2 %collective-permute-start.15 = (bf16[384,2048]{1,0:T(8,128)(2,1)}, bf16[384,2048]{1,0:T(8,128)(2,1)}, u32[]{:S(2)}, u32[]{:S(2)}) collective-permute-start(bf16[384,2048]{1,0:T(8,128)(2,1)} %get-tuple-element.166), channel_id=1, source_target_pairs={{0,4},{2,6},{4,0},{6,2},{8,12},{10,14},{12,8},{14,10},{1,5},{3,7},... | collective-permute-start | bytes 4718600 | tf_op jit(solution)/shard_map/ppermute | solution.py:683
  136.4 87.8 %collective-permute-start.18 = (bf16[2048,512]{1,0:T(8,128)(2,1)}, bf16[2048,512]{1,0:T(8,128)(2,1)}, u32[]{:S(2)}, u32[]{:S(2)}) collective-permute-start(bf16[2048,512]{1,0:T(8,128)(2,1)} %pad_maximum_fusion.5), channel_id=1, source_target_pairs={{4,8},{6,10},{8,4},{10,6},{5,9},{7,11},{9,5},{11,7},{20,24},{22,26... | collective-permute-start | bytes 6291464 | tf_op jit(solution)/shard_map/ppermute | solution.py:683
  152.9 62.1 %collective-permute-start.13 = (bf16[256,2048]{1,0:T(8,128)(2,1)}, bf16[256,2048]{1,0:T(8,128)(2,1)}, u32[]{:S(2)}, u32[]{:S(2)}) collective-permute-start(bf16[256,2048]{1,0:T(8,128)(2,1)} %get-tuple-element.163), channel_id=1, source_target_pairs={{0,4},{2,6},{12,8},{14,10},{1,5},{3,7},{13,9},{15,11},{16,20},{18,... | collective-permute-start | bytes 3145736 | tf_op jit(solution)/shard_map/ppermute | solution.py:683
  158.3 54.8 %collective-permute-start.11 = (bf16[1024,512]{1,0:T(8,128)(2,1)}, bf16[1024,512]{1,0:T(8,128)(2,1)}, u32[]{:S(2)}, u32[]{:S(2)}) collective-permute-start(bf16[1024,512]{1,0:T(8,128)(2,1)} %get-tuple-element.159), channel_id=1, source_target_pairs={{0,2},{2,0},{4,6},{6,4},{8,10},{10,8},{12,14},{14,12},{1,3},{3,1},... | collective-permute-start | bytes 3145736 | tf_op jit(solution)/shard_map/ppermute | solution.py:683
  187.3 234.5 %all-gather.17.cloned.1.call-start = ((), (), s32[]{:S(2)}) async-start(), calls=%async_computation.1 | async-start | bytes 9437184 | tf_op jit(solution)/shard_map/all_gather | solution.py:945
  224.2 48.2 %collective-permute-start.19 = (bf16[2048,512]{1,0:T(8,128)(2,1)}, bf16[2048,512]{1,0:T(8,128)(2,1)S(1)}, u32[]{:S(2)}, u32[]{:S(2)}) collective-permute-start(bf16[2048,512]{1,0:T(8,128)(2,1)} %pad_maximum_fusion.4), channel_id=1, source_target_pairs={{0,2},{2,0},{4,6},{6,4},{8,10},{10,8},{12,14},{14,12},{1,3},{3,1},... | collective-permute-start | bytes 6291464 | tf_op jit(solution)/shard_map/ppermute | solution.py:683
  225.7 85.7 %collective-permute-start.24 = (bf16[2048,512]{1,0:T(8,128)(2,1)}, bf16[2048,512]{1,0:T(8,128)(2,1)}, u32[]{:S(2)}, u32[]{:S(2)}) collective-permute-start(bf16[2048,512]{1,0:T(8,128)(2,1)} %collective-permute-done.18), channel_id=1, source_target_pairs={{4,0},{6,2},{8,12},{10,14},{5,1},{7,3},{9,13},{11,15},{20,16},{22,... | collective-permute-start | bytes 6291464 | tf_op jit(solution)/shard_map/ppermute | solution.py:683
  227.0 84.4 %collective-permute-start.22 = (bf16[2048,512]{1,0:T(8,128)(2,1)}, bf16[2048,512]{1,0:T(8,128)(2,1)}, u32[]{:S(2)}, u32[]{:S(2)}) collective-permute-start(bf16[2048,512]{1,0:T(8,128)(2,1)} %pad_maximum_fusion.4), channel_id=1, source_target_pairs={{4,8},{6,10},{8,4},{10,6},{5,9},{7,11},{9,5},{11,7},{20,24},{22,26... | collective-permute-start | bytes 6291464 | tf_op jit(solution)/shard_map/ppermute | solution.py:683
  232.9 76.3 %collective-permute-start.17 = (bf16[384,2048]{1,0:T(8,128)(2,1)S(1)}, bf16[384,2048]{1,0:T(8,128)(2,1)S(1)}, u32[]{:S(2)}, u32[]{:S(2)}) collective-permute-start(bf16[384,2048]{1,0:T(8,128)(2,1)S(1)} %get-tuple-element.168), channel_id=1, source_target_pairs={{0,4},{2,6},{4,0},{6,2},{8,12},{10,14},{12,8},{14,10},{1,5},{3,7},... | collective-permute-start | bytes 4718600 | tf_op jit(solution)/shard_map/ppermute | solution.py:683
  272.5 48.8 %collective-permute-start.20 = (bf16[512,2048]{1,0:T(8,128)(2,1)}, bf16[512,2048]{1,0:T(8,128)(2,1)}, u32[]{:S(2)}, u32[]{:S(2)}) collective-permute-start(bf16[512,2048]{1,0:T(8,128)(2,1)} %pad_maximum_fusion.3), channel_id=1, source_target_pairs={{0,2},{2,0},{4,6},{6,4},{8,10},{10,8},{12,14},{14,12},{1,3},{3,1},... | collective-permute-start | bytes 6291464 | tf_op jit(solution)/shard_map/ppermute | solution.py:683
  311.4 480.7 %all-gather.27.cloned.1.call-start = ((), (), s32[]{:S(2)}) async-start(), calls=%async_computation.7 | async-start | bytes 3145728 | tf_op jit(solution)/shard_map/all_gather | solution.py:1143
  316.4 48.7 %collective-permute-start.25 = (bf16[2048,512]{1,0:T(8,128)(2,1)}, bf16[2048,512]{1,0:T(8,128)(2,1)}, u32[]{:S(2)}, u32[]{:S(2)}) collective-permute-start(bf16[2048,512]{1,0:T(8,128)(2,1)} %get-tuple-element.176), channel_id=1, source_target_pairs={{0,2},{2,0},{4,6},{6,4},{8,10},{10,8},{12,14},{14,12},{1,3},{3,1},... | collective-permute-start | bytes 6291464 | tf_op jit(solution)/shard_map/ppermute | solution.py:683
  317.0 51.2 %collective-permute-start.23 = (bf16[512,2048]{1,0:T(8,128)(2,1)}, bf16[512,2048]{1,0:T(8,128)(2,1)}, u32[]{:S(2)}, u32[]{:S(2)}) collective-permute-start(bf16[512,2048]{1,0:T(8,128)(2,1)} %collective-permute-done.16), channel_id=1, source_target_pairs={{4,0},{6,2},{8,12},{10,14},{5,1},{7,3},{9,13},{11,15},{20,16},{22,... | collective-permute-start | bytes 6291464 | tf_op jit(solution)/shard_map/ppermute | solution.py:683
  321.3 46.9 %collective-permute-start.21 = (bf16[512,2048]{1,0:T(8,128)(2,1)}, bf16[512,2048]{1,0:T(8,128)(2,1)}, u32[]{:S(2)}, u32[]{:S(2)}) collective-permute-start(bf16[512,2048]{1,0:T(8,128)(2,1)} %pad_maximum_fusion.3), channel_id=1, source_target_pairs={{4,8},{6,10},{8,4},{10,6},{5,9},{7,11},{9,5},{11,7},{20,24},{22,26... | collective-permute-start | bytes 6291464 | tf_op jit(solution)/shard_map/ppermute | solution.py:683
  373.6 46.7 %collective-permute-start.26 = (bf16[512,2048]{1,0:T(8,128)(2,1)}, bf16[512,2048]{1,0:T(8,128)(2,1)S(1)}, u32[]{:S(2)}, u32[]{:S(2)}) collective-permute-start(bf16[512,2048]{1,0:T(8,128)(2,1)} %get-tuple-element.177), channel_id=1, source_target_pairs={{0,2},{2,0},{4,6},{6,4},{8,10},{10,8},{12,14},{14,12},{1,3},{3,1},... | collective-permute-start | bytes 6291464 | tf_op jit(solution)/shard_map/ppermute | solution.py:683
  467.8 48.3 %collective-permute-start.28 = (bf16[2048,512]{1,0:T(8,128)(2,1)}, bf16[2048,512]{1,0:T(8,128)(2,1)}, u32[]{:S(2)}, u32[]{:S(2)}) collective-permute-start(bf16[2048,512]{1,0:T(8,128)(2,1)} %convolution_convert_fusion.7), channel_id=1, source_target_pairs={{0,2},{2,0},{4,6},{6,4},{8,10},{10,8},{12,14},{14,12},{1,3},{3,1},... | collective-permute-start | bytes 6291464 | tf_op jit(solution)/shard_map/ppermute | solution.py:683
  488.9 36.8 %collective-permute-start.29 = (bf16[384,2048]{1,0:T(8,128)(2,1)S(1)}, bf16[384,2048]{1,0:T(8,128)(2,1)S(1)}, u32[]{:S(2)}, u32[]{:S(2)}) collective-permute-start(bf16[384,2048]{1,0:T(8,128)(2,1)S(1)} %add_convert_fusion.2), channel_id=1, source_target_pairs={{0,4},{2,6},{4,0},{6,2},{8,12},{10,14},{12,8},{14,10},{1,5},{3,7},... | collective-permute-start | bytes 4718600 | tf_op jit(solution)/shard_map/ppermute | solution.py:731
  532.4 48.7 %collective-permute-start.31 = (bf16[2048,512]{1,0:T(8,128)(2,1)}, bf16[2048,512]{1,0:T(8,128)(2,1)}, u32[]{:S(2)}, u32[]{:S(2)}) collective-permute-start(bf16[2048,512]{1,0:T(8,128)(2,1)} %convolution_convert_fusion.6), channel_id=1, source_target_pairs={{0,2},{2,0},{4,6},{6,4},{8,10},{10,8},{12,14},{14,12},{1,3},{3,1},... | collective-permute-start | bytes 6291464 | tf_op jit(solution)/shard_map/ppermute | solution.py:683
  536.2 93.3 %collective-permute-start.37 = (bf16[2048,512]{1,0:T(8,128)(2,1)}, bf16[2048,512]{1,0:T(8,128)(2,1)}, u32[]{:S(2)}, u32[]{:S(2)}) collective-permute-start(bf16[2048,512]{1,0:T(8,128)(2,1)} %add_convert_fusion.1), channel_id=1, source_target_pairs={{0,4},{2,6},{12,8},{14,10},{1,5},{3,7},{13,9},{15,11},{16,20},{18,... | collective-permute-start | bytes 6291464 | tf_op jit(solution)/shard_map/ppermute | solution.py:683
  541.5 81.2 %collective-permute-start.33 = (bf16[2048,512]{1,0:T(8,128)(2,1)}, bf16[2048,512]{1,0:T(8,128)(2,1)}, u32[]{:S(2)}, u32[]{:S(2)}) collective-permute-start(bf16[2048,512]{1,0:T(8,128)(2,1)} %add_convert_fusion.1), channel_id=1, source_target_pairs={{4,8},{6,10},{8,4},{10,6},{5,9},{7,11},{9,5},{11,7},{20,24},{22,26... | collective-permute-start | bytes 6291464 | tf_op jit(solution)/shard_map/ppermute | solution.py:683
  543.5 146.9 %collective-permute-start.35 = (bf16[512,2048]{1,0:T(8,128)(2,1)}, bf16[512,2048]{1,0:T(8,128)(2,1)}, u32[]{:S(2)}, u32[]{:S(2)}) collective-permute-start(bf16[512,2048]{1,0:T(8,128)(2,1)} %convolution_convert_fusion.4), channel_id=1, source_target_pairs={{0,2},{2,0},{4,6},{6,4},{8,10},{10,8},{12,14},{14,12},{1,3},{3,1},... | collective-permute-start | bytes 6291464 | tf_op jit(solution)/shard_map/ppermute | solution.py:683
  545.2 125.5 %collective-permute-start.34 = (bf16[512,2048]{1,0:T(8,128)(2,1)}, bf16[512,2048]{1,0:T(8,128)(2,1)}, u32[]{:S(2)}, u32[]{:S(2)}) collective-permute-start(bf16[512,2048]{1,0:T(8,128)(2,1)} %convolution_convert_fusion.5), channel_id=1, source_target_pairs={{0,2},{2,0},{4,6},{6,4},{8,10},{10,8},{12,14},{14,12},{1,3},{3,1},... | collective-permute-start | bytes 6291464 | tf_op jit(solution)/shard_map/ppermute | solution.py:683
  622.7 67.8 %collective-permute-start.36 = (bf16[384,2048]{1,0:T(8,128)(2,1)S(1)}, bf16[384,2048]{1,0:T(8,128)(2,1)S(1)}, u32[]{:S(2)}, u32[]{:S(2)}) collective-permute-start(bf16[384,2048]{1,0:T(8,128)(2,1)S(1)} %convolution_convert_fusion.9), channel_id=1, source_target_pairs={{0,1},{1,0},{2,3},{3,2},{4,5},{5,4},{6,7},{7,6},{8,9},{9,8},{10,11... | collective-permute-start | bytes 4718600 | tf_op jit(solution)/shard_map/ppermute | solution.py:728
  629.5 72.3 %collective-permute-start.38 = (bf16[2048,512]{1,0:T(8,128)(2,1)}, bf16[2048,512]{1,0:T(8,128)(2,1)}, u32[]{:S(2)}, u32[]{:S(2)}) collective-permute-start(bf16[2048,512]{1,0:T(8,128)(2,1)} %collective-permute-done.37), channel_id=1, source_target_pairs={{4,8},{6,10},{8,4},{10,6},{5,9},{7,11},{9,5},{11,7},{20,24},{22,26... | collective-permute-start | bytes 6291464 | tf_op jit(solution)/shard_map/ppermute | solution.py:683
  677.1 50.0 %collective-permute-start.51 = (bf16[512,2048]{1,0:T(8,128)(2,1)}, bf16[512,2048]{1,0:T(8,128)(2,1)}, u32[]{:S(2)}, u32[]{:S(2)}) collective-permute-start(bf16[512,2048]{1,0:T(8,128)(2,1)} %add_convert_fusion), channel_id=1, source_target_pairs={{0,4},{2,6},{12,8},{14,10},{1,5},{3,7},{13,9},{15,11},{16,20},{18,... | collective-permute-start | bytes 6291464 | tf_op jit(solution)/shard_map/ppermute | solution.py:683
  707.2 67.5 %collective-permute-start.41 = (bf16[1024,512]{1,0:T(8,128)(2,1)}, bf16[1024,512]{1,0:T(8,128)(2,1)}, u32[]{:S(2)}, u32[]{:S(2)}) collective-permute-start(bf16[1024,512]{1,0:T(8,128)(2,1)} %convolution_convert_fusion.16), channel_id=1, source_target_pairs={{0,2},{2,0},{4,6},{6,4},{8,10},{10,8},{12,14},{14,12},{1,3},{3,1},... | collective-permute-start | bytes 3145736 | tf_op jit(solution)/shard_map/ppermute | solution.py:683
  707.7 74.0 %collective-permute-start.61 = (bf16[2048,256]{1,0:T(8,128)(2,1)}, bf16[2048,256]{1,0:T(8,128)(2,1)}, u32[]{:S(2)}, u32[]{:S(2)}) collective-permute-start(bf16[2048,256]{1,0:T(8,128)(2,1)} %fusion.8), channel_id=1, source_target_pairs={{0,4},{2,6},{4,0},{6,2},{8,12},{10,14},{12,8},{14,10},{1,5},{3,7},... | collective-permute-start | bytes 3145736 | tf_op jit(solution)/shard_map/ppermute | solution.py:683
  711.3 56.7 %collective-permute-start.40 = (bf16[512,2048]{1,0:T(8,128)(2,1)}, bf16[512,2048]{1,0:T(8,128)(2,1)}, u32[]{:S(2)}, u32[]{:S(2)}) collective-permute-start(bf16[512,2048]{1,0:T(8,128)(2,1)} %add_convert_fusion), channel_id=1, source_target_pairs={{4,8},{6,10},{8,4},{10,6},{5,9},{7,11},{9,5},{11,7},{20,24},{22,26... | collective-permute-start | bytes 6291464 | tf_op jit(solution)/shard_map/ppermute | solution.py:683
  727.1 65.0 %collective-permute-start.42 = (bf16[512,1024]{1,0:T(8,128)(2,1)}, bf16[512,1024]{1,0:T(8,128)(2,1)}, u32[]{:S(2)}, u32[]{:S(2)}) collective-permute-start(bf16[512,1024]{1,0:T(8,128)(2,1)} %convolution_convert_fusion.14), channel_id=1, source_target_pairs={{0,2},{2,0},{4,6},{6,4},{8,10},{10,8},{12,14},{14,12},{1,3},{3,1},... | collective-permute-start | bytes 3145736 | tf_op jit(solution)/shard_map/ppermute | solution.py:683
  732.4 75.1 %collective-permute-start.52 = (bf16[512,2048]{1,0:T(8,128)(2,1)}, bf16[512,2048]{1,0:T(8,128)(2,1)}, u32[]{:S(2)}, u32[]{:S(2)}) collective-permute-start(bf16[512,2048]{1,0:T(8,128)(2,1)} %collective-permute-done.51), channel_id=1, source_target_pairs={{4,8},{6,10},{8,4},{10,6},{5,9},{7,11},{9,5},{11,7},{20,24},{22,26... | collective-permute-start | bytes 6291464 | tf_op jit(solution)/shard_map/ppermute | solution.py:683
  749.1 102.1 %all-gather.29.cloned.1.call-start = ((), (), s32[]{:S(2)}) async-start(), calls=%async_computation.8 | async-start | bytes 3145728 | tf_op jit(solution)/shard_map/all_gather | solution.py:1143
  792.1 94.4 %all-gather.31.cloned.1.call-start = ((), (), s32[]{:S(2)}) async-start(), calls=%async_computation.9 | async-start | bytes 3145728 | tf_op jit(solution)/shard_map/all_gather | solution.py:1143
  851.2 70.1 %reduce-scatter.2.cloned.1.call-start = ((), (), s32[]{:S(2)}) async-start(), calls=%async_computation.3 | async-start | bytes 9437184 | tf_op jit(solution)/shard_map/reduce_scatter | solution.py:1095
  851.8 89.6 %all-gather.33.cloned.1.call-start = ((), (), s32[]{:S(2)}) async-start(), calls=%async_computation.10 | async-start | bytes 3145728 | tf_op jit(solution)/shard_map/all_gather | solution.py:1143
  886.4 152.6 %all-gather.23.cloned.1.call-start = ((), (), s32[]{:S(2)}) async-start(), calls=%async_computation.5 | async-start | bytes 4718592 | tf_op jit(solution)/shard_map/all_gather | solution.py:945
  887.0 166.4 %all-gather.35.cloned.1.call-start = ((), (), s32[]{:S(2)}) async-start(), calls=%async_computation.11 | async-start | bytes 1572864 | tf_op jit(solution)/shard_map/all_gather | solution.py:1143
  888.4 43.1 %collective-permute-start.56 = (bf16[512,1024]{1,0:T(8,128)(2,1)}, bf16[512,1024]{1,0:T(8,128)(2,1)}, u32[]{:S(2)}, u32[]{:S(2)}) collective-permute-start(bf16[512,1024]{1,0:T(8,128)(2,1)} %convolution_convert_fusion.13), channel_id=1, source_target_pairs={{0,2},{2,0},{4,6},{6,4},{8,10},{10,8},{12,14},{14,12},{1,3},{3,1},... | collective-permute-start | bytes 3145736 | tf_op jit(solution)/shard_map/ppermute | solution.py:683
  889.9 41.5 %collective-permute-start.57 = (bf16[512,1024]{1,0:T(8,128)(2,1)}, bf16[512,1024]{1,0:T(8,128)(2,1)}, u32[]{:S(2)}, u32[]{:S(2)}) collective-permute-start(bf16[512,1024]{1,0:T(8,128)(2,1)} %add.296), channel_id=1, source_target_pairs={{4,8},{6,10},{8,4},{10,6},{5,9},{7,11},{9,5},{11,7},{20,24},{22,26... | collective-permute-start | bytes 3145736 | tf_op jit(solution)/shard_map/ppermute | solution.py:683
  924.2 37.1 %collective-permute-start.44 = (bf16[384,2048]{1,0:T(8,128)(2,1)}, bf16[384,2048]{1,0:T(8,128)(2,1)}, u32[]{:S(2)}, u32[]{:S(2)}) collective-permute-start(bf16[384,2048]{1,0:T(8,128)(2,1)} %slice.309), channel_id=1, source_target_pairs={{0,4},{2,6},{4,0},{6,2},{8,12},{10,14},{12,8},{14,10},{1,5},{3,7},... | collective-permute-start | bytes 4718600 | tf_op jit(solution)/shard_map/ppermute | solution.py:683
  941.5 115.3 %all-gather.21.cloned.1.call-start = ((), (), s32[]{:S(2)}) async-start(), calls=%async_computation.4 | async-start | bytes 4718592 | tf_op jit(solution)/shard_map/all_gather | solution.py:945
  992.4 45.7 %collective-permute-start.67 = (bf16[267,128]{1,0:T(8,128)(2,1)S(1)}, bf16[267,128]{1,0:T(8,128)(2,1)S(1)}, u32[]{:S(2)}, u32[]{:S(2)}) collective-permute-start(bf16[267,128]{1,0:T(8,128)(2,1)S(1)} %get-tuple-element.386), channel_id=1, source_target_pairs={{0,16},{16,0},{1,17},{17,1},{2,18},{18,2},{3,19},{19,3},{4,20},{20... | collective-permute-start | bytes 205064 | tf_op jit(solution)/shard_map/ppermute | solution.py:1172
  (111 other events, 2016.7 us)
Sparse Core Ops, SparseCore 0:
  35.5 49.0 all-gather.24
  749.2 31.9 all-gather.26
  792.2 31.5 all-gather.28
  851.4 31.6 all-gather.30
  886.6 31.9 all-gather.32
  919.9 12.1 all-gather.22
  941.6 22.5 all-gather.34
  966.4 12.1 all-gather.20
Sparse Core Ops, SparseCore 1:
  187.4 16.4 all-gather.18
  311.4 15.4 all-gather.16
  854.0 12.9 reduce-scatter.1
